TPU v7x, 256 devices: a whole 4x4x8 slice. The times are simulated.
256 devices in a mesh: gx: 8 (over z), gy: 32 (over y, x, core).
Axes of the slice: x: 4, y: 4, z: 8, core: 2. Of those that a mesh axis runs over, the one named last changes fastest.
Arguments:
- populations: float32 [2, 7, 128, 256, 512], P(None, None, 'gx', 'gy'), may hold values from 0.02 to 0.3
- conductivity: float32 [128, 256, 512], P('gx', 'gy'), may hold values from 0.5 to 4
- deposit_mask: int32 [128, 256, 512], P('gx', 'gy'), may hold values 0 or 1
- electrode_flags: int32 [128, 256, 512], P('gx', 'gy'), may hold values 0 or 1
- previous_potential: float32 [128, 256, 512], P('gx', 'gy'), may hold values from -9 to 9
Outputs:
- potential: float32 [128, 256, 512], P('gx', 'gy')
- populations_next: float32 [2, 7, 128, 256, 512], P(None, None, 'gx', 'gy')
All inputs are finite; a program needn't handle non-finite values. No bound on the sum of `deposit_mask` or of `electrode_flags` on one device may be relied on, other than what follows from the above.
Results may differ from a plain program's by a relative error of at most 0.0003.
Values sent between devices are 32-bit elements; how exact they have to be, the bound alone decides.
No kernel may reach another device: no remote copies, remote signals or barrier semaphores. Data moves between devices by JAX's collectives and lax.ppermute only.
A program may use at most 128 MiB of HBM per device.

v0:
```python
import jax
import jax.numpy as jnp
from jax import lax
from jax.sharding import PartitionSpec as P

ITERS = 3


SCREEN_RATE = 0.01
WEIGHTS = (0.25, 0.125, 0.125, 0.125, 0.125, 0.125, 0.125)
OPPOSITE = (0, 2, 1, 4, 3, 6, 5)
DRIFT_COEF = (-0.02, 0.016)
RELAX_TIME = (0.8, 1.1)


def padded_2(cells, sides, width):
    for axis, dim in sides:
        count = lax.axis_size(axis)
        head = lax.slice_in_dim(cells, 0, width, axis=dim)
        tail = lax.slice_in_dim(cells, cells.shape[dim] - width, cells.shape[dim], axis=dim)
        cells = jnp.concatenate(
            [
                lax.ppermute(tail, axis, [(i, (i + 1) % count) for i in range(count)]),
                cells,
                lax.ppermute(head, axis, [((i + 1) % count, i) for i in range(count)]),
            ],
            axis=dim,
        )
    return cells


def from_behind(block, axis, distance):
    devices = range(lax.axis_size(axis))
    route = [((i - distance) % len(devices), i) for i in devices]
    return lax.ppermute(block, axis, route)


def harmonic(left_cell, right_cell):
    return 2.0 * left_cell * right_cell / (left_cell + right_cell)


def harmonic_faces(sigma_pad):
    middle = sigma_pad[1:-1, 1:-1]
    upper_z = jnp.concatenate([middle[:, :, 1:], middle[:, :, -1:]], axis=2)
    lower_z = jnp.concatenate([middle[:, :, :1], middle[:, :, :-1]], axis=2)
    return (
        harmonic(middle, sigma_pad[2:, 1:-1]),
        harmonic(middle, sigma_pad[:-2, 1:-1]),
        harmonic(middle, sigma_pad[1:-1, 2:]),
        harmonic(middle, sigma_pad[1:-1, :-2]),
        harmonic(middle, upper_z),
        harmonic(middle, lower_z),
    )


def laplace(padded, weights):
    middle = padded[1:-1, 1:-1]
    zero_layer = jnp.zeros_like(middle[:, :, :1])
    above_z = jnp.concatenate([middle[:, :, 1:], zero_layer], axis=2)
    below_z = jnp.concatenate([zero_layer, middle[:, :, :-1]], axis=2)
    summed = weights[0] * (middle - padded[2:, 1:-1]) + weights[1] * (middle - padded[:-2, 1:-1])
    summed = (
        summed
        + weights[2] * (middle - padded[1:-1, 2:])
        + weights[3] * (middle - padded[1:-1, :-2])
    )
    summed = summed + weights[4] * (middle - above_z) + weights[5] * (middle - below_z)
    return summed + SCREEN_RATE * middle


def collide(populations_in, potential_pad):
    middle = potential_pad[1:-1, 1:-1]
    zero_layer = jnp.zeros_like(middle[:, :, :1])
    grad_x = 0.5 * (potential_pad[2:, 1:-1] - potential_pad[:-2, 1:-1])
    grad_y = 0.5 * (potential_pad[1:-1, 2:] - potential_pad[1:-1, :-2])
    grad_z = 0.5 * (
        jnp.concatenate([middle[:, :, 1:], zero_layer], axis=2)
        - jnp.concatenate([zero_layer, middle[:, :, :-1]], axis=2)
    )
    density = jnp.sum(populations_in, axis=1)
    collided = []
    for species in range(2):
        velo_x = DRIFT_COEF[species] * grad_x
        velo_y = DRIFT_COEF[species] * grad_y
        velo_z = DRIFT_COEF[species] * grad_z
        projected = (None, velo_x, -velo_x, velo_y, -velo_y, velo_z, -velo_z)
        relax_rate = 1.0 / RELAX_TIME[species]
        out_rows = []
        for lattice_dir in range(7):
            if lattice_dir == 0:
                balance = WEIGHTS[0] * density[species]
            else:
                balance = (
                    WEIGHTS[lattice_dir] * density[species] * (1.0 + 4.0 * projected[lattice_dir])
                )
            current = populations_in[species, lattice_dir]
            out_rows.append(current - relax_rate * (current - balance))
        collided.append(jnp.stack(out_rows, axis=0))
    return jnp.stack(collided, axis=0)


def stream(collided_pad, solid_pad):
    middle = collided_pad[:, :, 1:-1, 1:-1]
    solid_mid = solid_pad[1:-1, 1:-1]
    zero_layer = jnp.zeros_like(middle[:, 0, :, :, :1])
    one_layer = jnp.ones_like(solid_mid[:, :, :1])
    sources = (
        (collided_pad[:, 1, :-2, 1:-1], solid_pad[:-2, 1:-1]),
        (collided_pad[:, 2, 2:, 1:-1], solid_pad[2:, 1:-1]),
        (collided_pad[:, 3, 1:-1, :-2], solid_pad[1:-1, :-2]),
        (collided_pad[:, 4, 1:-1, 2:], solid_pad[1:-1, 2:]),
        (
            jnp.concatenate([zero_layer, middle[:, 5, :, :, :-1]], axis=3),
            jnp.concatenate([one_layer, solid_mid[:, :, :-1]], axis=2),
        ),
        (
            jnp.concatenate([middle[:, 6, :, :, 1:], zero_layer], axis=3),
            jnp.concatenate([solid_mid[:, :, 1:], one_layer], axis=2),
        ),
    )
    arrived = [middle[:, 0]]
    for lattice_dir in range(1, 7):
        source, blocked = sources[lattice_dir - 1]
        arrived.append(jnp.where(blocked > 0.5, middle[:, OPPOSITE[lattice_dir]], source))
    return jnp.stack(arrived, axis=1) * (1.0 - solid_mid)


def squares_sum(residual):
    return lax.psum(jnp.sum(residual * residual), ("gx", "gy"))


def local(populations, conductivity, deposit_mask, electrode_flags, previous_potential):
    solid_cell = deposit_mask.astype(jnp.float32)
    sigma_cell = conductivity * (1.0 + 3.0 * solid_cell)
    pinned = electrode_flags.astype(jnp.float32)
    unknown = 1.0 - pinned
    sigma_pad, solid_pad, previous_pad = (
        padded_2(sigma_cell, (("gx", 0), ("gy", 1)), 1),
        padded_2(solid_cell, (("gx", 0), ("gy", 1)), 1),
        padded_2(previous_potential, (("gx", 0), ("gy", 1)), 1),
    )
    weights = harmonic_faces(sigma_pad)
    density = jnp.sum(populations, axis=1)
    charge = 2.0 * density[0] - 2.0 * density[1]
    residual = unknown * (charge - laplace(previous_pad, weights))
    correction = jnp.zeros_like(residual)
    direction = residual
    norm_now = squares_sum(residual)
    for sweep in range(ITERS):
        padded = padded_2(unknown * direction, (("gx", 0), ("gy", 1)), 1)
        mapped = unknown * laplace(padded, weights) + pinned * direction
        step_size = norm_now / lax.psum(jnp.sum(direction * mapped), ("gx", "gy"))
        correction = correction + step_size * direction
        residual = residual - step_size * mapped
        if sweep + 1 < ITERS:
            norm_next = squares_sum(residual)
            direction = residual + norm_next / norm_now * direction
            norm_now = norm_next
    potential = previous_potential + correction
    potential_pad = padded_2(potential, (("gx", 0), ("gy", 1)), 1)
    collided = collide(populations, potential_pad)
    lower_rows = from_behind(collided[:, 1, -1:], "gx", 1)
    upper_rows = from_behind(collided[:, 2, :1], "gx", -1)
    lower_cols = from_behind(collided[:, 3, :, -1:], "gy", 1)
    upper_cols = from_behind(collided[:, 4, :, :1], "gy", -1)
    collided_pad = jnp.pad(collided, ((0, 0), (0, 0), (1, 1), (1, 1), (0, 0)))
    collided_pad = collided_pad.at[:, 1, :1, 1:-1].set(lower_rows)
    collided_pad = collided_pad.at[:, 2, -1:, 1:-1].set(upper_rows)
    collided_pad = collided_pad.at[:, 3, 1:-1, :1].set(lower_cols)
    collided_pad = collided_pad.at[:, 4, 1:-1, -1:].set(upper_cols)
    return (potential, stream(collided_pad, solid_pad))


def solution(mesh):
    in_specs = (
        P(None, None, "gx", "gy", None),
        P("gx", "gy", None),
        P("gx", "gy", None),
        P("gx", "gy", None),
        P("gx", "gy", None),
    )
    out_specs = (P("gx", "gy", None), P(None, None, "gx", "gy", None))
    return jax.shard_map(local, mesh=mesh, in_specs=in_specs, out_specs=out_specs, check_vma=False)
```

profile of v0, /device:TPU:0, one launch (start us, length us, event | category | flops | bytes accessed | tf_op | source)
XLA Modules:
  0.0 518.1 jit_solution(9784969333083770036)
XLA Ops:
  0.6 1.8 broadcast_subtract_fusion
  2.5 4.1 collective-permute-start
  7.4 3.2 collective-permute-start.1
  13.5 3.9 collective-permute-start.4
  17.5 5.1 collective-permute-start.5
  22.8 2.5 reduce_sum.67
  25.3 3.0 collective-permute-start.29
  30.1 3.0 collective-permute-start.8
  34.5 3.5 collective-permute-done.9
  39.8 5.6 %collective-permute-done.11 = f32[18,1,512]{2,1,0:T(1,128)S(1)} collective-permute-done((f32[18,1,512]{2,1,0:T(1,128)S(1)}, f32[18,1,512]{2,1,0:T(1,128)S(1)}, u32[]{:S(2)}, u32[]{:S(2)}) %collective-permute-start.11) | collective-permute-done | bytes 36896 | tf_op jit(solution)/shard_map/ppermute | solution.py:23
  45.4 2.0 multiply_reduce_fusion.3
  47.4 71.2 %all-reduce.15 = (f32[]{:T(128)}, f32[]{:T(128)}) all-reduce(f32[]{:T(128)} %get-tuple-element.51, f32[]{:T(128)} %get-tuple-element.50), channel_id=1, replica_groups=mesh['gx'=8,'gy'=32] {'gx','gy'}, use_global_device_ids=true, to_apply=%region_2.0 | all-reduce | flops 2 | bytes 16 | tf_op jit(solution)/shard_map/psum | solution.py:129
  119.8 2.4 multiply_reduce_fusion.2
  122.3 74.5 %psum.44 = f32[]{:T(128)} all-reduce(f32[]{:T(128)} %get-tuple-element.62), channel_id=1, replica_groups=mesh['gx'=8,'gy'=32] {'gx','gy'}, use_global_device_ids=true, to_apply=%region_6.0 | all-reduce | flops 1 | bytes 8 | tf_op jit(solution)/shard_map/psum | solution.py:129
  203.2 2.4 collective-permute-done.13
  207.4 5.1 collective-permute-done.15
  212.5 1.9 multiply_reduce_fusion.1
  214.5 71.9 %psum.45 = f32[]{:T(128)} all-reduce(f32[]{:T(128)} %get-tuple-element.58), channel_id=1, replica_groups=mesh['gx'=8,'gy'=32] {'gx','gy'}, use_global_device_ids=true, to_apply=%region_8.0 | all-reduce | flops 1 | bytes 8 | tf_op jit(solution)/shard_map/psum | solution.py:152
  291.4 73.9 %psum.46 = f32[]{:T(128)} all-reduce(f32[]{:T(128)} %multiply_reduce_fusion), channel_id=1, replica_groups=mesh['gx'=8,'gy'=32] {'gx','gy'}, use_global_device_ids=true, to_apply=%region_10.0 | all-reduce | flops 1 | bytes 8 | tf_op jit(solution)/shard_map/psum | solution.py:129
  370.2 5.1 collective-permute-start.31
  377.2 5.1 collective-permute-done.19
  382.3 2.3 fusion.115
  384.8 72.5 %psum.47 = f32[]{:T(128)} all-reduce(f32[]{:T(128)} %fusion.115), channel_id=1, replica_groups=mesh['gx'=8,'gy'=32] {'gx','gy'}, use_global_device_ids=true, to_apply=%region_12.0 | all-reduce | flops 1 | bytes 8 | tf_op jit(solution)/shard_map/psum | solution.py:152
  464.0 2.0 collective-permute-done.21
  468.0 5.1 collective-permute-done.23
  474.7 3.2 collective-permute-start.25
  477.8 4.6 collective-permute-start.27
  482.9 4.2 pad.34
  489.9 2.1 scatter.16
  492.0 8.5 %copy.9 = f32[2,7,18,10,512]{4,3,2,0,1:T(8,128)} copy(f32[2,7,18,10,512]{4,3,2,1,0:T(8,128)} %scatter.16) | data formatting | bytes 10321920 | tf_op jit(solution)/shard_map/scatter | solution.py:169
  500.5 2.1 scatter.19
  515.6 2.3 broadcast_multiply_fusion
  (130 shorter events, 49.9 us)
Async XLA Ops:
  2.5 11.0 %collective-permute-start = (f32[1,8,512]{2,1,0:T(8,128)S(1)}, f32[1,8,512]{2,1,0:T(8,128)S(1)}, u32[]{:S(2)}, u32[]{:S(2)}) collective-permute-start(f32[1,8,512]{2,1,0:T(8,128)S(1)} %get-tuple-element.129), channel_id=1, source_target_pairs={{32,0},{64,32},{96,64},{128,96},{160,128},{192,160},{224,192},{0,2... | collective-permute-start | bytes 49160 | tf_op jit(solution)/shard_map/ppermute | solution.py:25
  6.6 6.9 %collective-permute-start.2 = (f32[1,8,512]{2,1,0:T(8,128)S(1)}, f32[1,8,512]{2,1,0:T(8,128)S(1)}, u32[]{:S(2)}, u32[]{:S(2)}) collective-permute-start(f32[1,8,512]{2,1,0:T(8,128)S(1)} %get-tuple-element.128), channel_id=1, source_target_pairs={{0,32},{32,64},{64,96},{96,128},{128,160},{160,192},{192,224},{224... | collective-permute-start | bytes 49160 | tf_op jit(solution)/shard_map/ppermute | solution.py:23
  7.3 10.1 %collective-permute-start.3 = (f32[1,8,512]{2,1,0:T(8,128)S(1)}, f32[1,8,512]{2,1,0:T(8,128)S(1)}, u32[]{:S(2)}, u32[]{:S(2)}) collective-permute-start(f32[1,8,512]{2,1,0:T(8,128)S(1)} %get-tuple-element.131), channel_id=1, source_target_pairs={{0,32},{32,64},{64,96},{96,128},{128,160},{160,192},{192,224},{224... | collective-permute-start | bytes 49160 | tf_op jit(solution)/shard_map/ppermute | solution.py:23
  7.4 10.1 %collective-permute-start.1 = (f32[1,8,512]{2,1,0:T(8,128)S(1)}, f32[1,8,512]{2,1,0:T(8,128)S(1)}, u32[]{:S(2)}, u32[]{:S(2)}) collective-permute-start(f32[1,8,512]{2,1,0:T(8,128)S(1)} %get-tuple-element.130), channel_id=1, source_target_pairs={{32,0},{64,32},{96,64},{128,96},{160,128},{192,160},{224,192},{0,2... | collective-permute-start | bytes 49160 | tf_op jit(solution)/shard_map/ppermute | solution.py:25
  12.2 357.9 %collective-permute-start.28 = (f32[1,8,512]{2,1,0:T(8,128)}, f32[1,8,512]{2,1,0:T(8,128)S(1)}, u32[]{:S(2)}, u32[]{:S(2)}) collective-permute-start(f32[1,8,512]{2,1,0:T(8,128)} %get-tuple-element.107), channel_id=1, source_target_pairs={{0,32},{32,64},{64,96},{96,128},{128,160},{160,192},{192,224},{224... | collective-permute-start | bytes 49160 | tf_op jit(solution)/shard_map/ppermute | solution.py:23
  13.5 11.7 %collective-permute-start.4 = (f32[18,1,512]{2,1,0:T(1,128)S(1)}, f32[18,1,512]{2,1,0:T(1,128)S(1)}, u32[]{:S(2)}, u32[]{:S(2)}) collective-permute-start(f32[18,1,512]{2,1,0:T(1,128)S(1)} %get-tuple-element.96), channel_id=1, source_target_pairs={{1,0},{2,1},{3,2},{4,3},{5,4},{6,5},{7,6},{8,7},{9,8},{10,9},{11,1... | collective-permute-start | bytes 110600 | tf_op jit(solution)/shard_map/ppermute | solution.py:25
  17.4 10.8 %collective-permute-start.6 = (f32[18,1,512]{2,1,0:T(1,128)S(1)}, f32[18,1,512]{2,1,0:T(1,128)S(1)}, u32[]{:S(2)}, u32[]{:S(2)}) collective-permute-start(f32[18,1,512]{2,1,0:T(1,128)S(1)} %get-tuple-element.97), channel_id=1, source_target_pairs={{0,1},{1,2},{2,3},{3,4},{4,5},{5,6},{6,7},{7,8},{8,9},{9,10},{10,1... | collective-permute-start | bytes 110600 | tf_op jit(solution)/shard_map/ppermute | solution.py:23
  17.5 10.7 %collective-permute-start.5 = (f32[18,1,512]{2,1,0:T(1,128)S(1)}, f32[18,1,512]{2,1,0:T(1,128)S(1)}, u32[]{:S(2)}, u32[]{:S(2)}) collective-permute-start(f32[18,1,512]{2,1,0:T(1,128)S(1)} %get-tuple-element.98), channel_id=1, source_target_pairs={{1,0},{2,1},{3,2},{4,3},{5,4},{6,5},{7,6},{8,7},{9,8},{10,9},{11,1... | collective-permute-start | bytes 110600 | tf_op jit(solution)/shard_map/ppermute | solution.py:25
  22.7 6.7 %collective-permute-start.7 = (f32[18,1,512]{2,1,0:T(1,128)S(1)}, f32[18,1,512]{2,1,0:T(1,128)S(1)}, u32[]{:S(2)}, u32[]{:S(2)}) collective-permute-start(f32[18,1,512]{2,1,0:T(1,128)S(1)} %get-tuple-element.99), channel_id=1, source_target_pairs={{0,1},{1,2},{2,3},{3,4},{4,5},{5,6},{6,7},{7,8},{8,9},{9,10},{10,1... | collective-permute-start | bytes 110600 | tf_op jit(solution)/shard_map/ppermute | solution.py:23
  25.3 344.8 %collective-permute-start.29 = (f32[1,8,512]{2,1,0:T(8,128)}, f32[1,8,512]{2,1,0:T(8,128)S(1)}, u32[]{:S(2)}, u32[]{:S(2)}) collective-permute-start(f32[1,8,512]{2,1,0:T(8,128)} %get-tuple-element.106), channel_id=1, source_target_pairs={{32,0},{64,32},{96,64},{128,96},{160,128},{192,160},{224,192},{0,2... | collective-permute-start | bytes 49160 | tf_op jit(solution)/shard_map/ppermute | solution.py:25
  30.1 4.4 collective-permute-start.8
  33.1 4.9 collective-permute-start.9
  38.1 1.7 collective-permute-start.10
  38.2 7.2 %collective-permute-start.11 = (f32[18,1,512]{2,1,0:T(1,128)S(1)}, f32[18,1,512]{2,1,0:T(1,128)S(1)}, u32[]{:S(2)}, u32[]{:S(2)}) collective-permute-start(f32[18,1,512]{2,1,0:T(1,128)S(1)} %get-tuple-element.95), channel_id=1, source_target_pairs={{0,1},{1,2},{2,3},{3,4},{4,5},{5,6},{6,7},{7,8},{8,9},{9,10},{10,1... | collective-permute-start | bytes 110600 | tf_op jit(solution)/shard_map/ppermute | solution.py:23
  199.3 3.8 collective-permute-start.12
  200.6 4.9 collective-permute-start.13
  205.6 1.9 collective-permute-start.14
  205.8 6.7 %collective-permute-start.15 = (f32[18,1,512]{2,1,0:T(1,128)S(1)}, f32[18,1,512]{2,1,0:T(1,128)S(1)}, u32[]{:S(2)}, u32[]{:S(2)}) collective-permute-start(f32[18,1,512]{2,1,0:T(1,128)S(1)} %get-tuple-element.93), channel_id=1, source_target_pairs={{0,1},{1,2},{2,3},{3,4},{4,5},{5,6},{6,7},{7,8},{8,9},{9,10},{10,1... | collective-permute-start | bytes 110600 | tf_op jit(solution)/shard_map/ppermute | solution.py:23
  367.9 7.3 %collective-permute-start.16 = (f32[1,8,512]{2,1,0:T(8,128)S(1)}, f32[1,8,512]{2,1,0:T(8,128)S(1)}, u32[]{:S(2)}, u32[]{:S(2)}) collective-permute-start(f32[1,8,512]{2,1,0:T(8,128)S(1)} %get-tuple-element.113), channel_id=1, source_target_pairs={{32,0},{64,32},{96,64},{128,96},{160,128},{192,160},{224,192},{0,2... | collective-permute-start | bytes 49160 | tf_op jit(solution)/shard_map/ppermute | solution.py:25
  369.3 6.0 %collective-permute-start.17 = (f32[1,8,512]{2,1,0:T(8,128)S(1)}, f32[1,8,512]{2,1,0:T(8,128)S(1)}, u32[]{:S(2)}, u32[]{:S(2)}) collective-permute-start(f32[1,8,512]{2,1,0:T(8,128)S(1)} %get-tuple-element.112), channel_id=1, source_target_pairs={{0,32},{32,64},{64,96},{96,128},{128,160},{160,192},{192,224},{224... | collective-permute-start | bytes 49160 | tf_op jit(solution)/shard_map/ppermute | solution.py:23
  370.1 14.5 %collective-permute-start.30 = (f32[18,1,512]{2,1,0:T(1,128)S(1)}, f32[18,1,512]{2,1,0:T(1,128)S(1)}, u32[]{:S(2)}, u32[]{:S(2)}) collective-permute-start(f32[18,1,512]{2,1,0:T(1,128)S(1)} %get-tuple-element.87), channel_id=1, source_target_pairs={{0,1},{1,2},{2,3},{3,4},{4,5},{5,6},{6,7},{7,8},{8,9},{9,10},{10,1... | collective-permute-start | bytes 110600 | tf_op jit(solution)/shard_map/ppermute | solution.py:23
  370.2 14.4 %collective-permute-start.31 = (f32[18,1,512]{2,1,0:T(1,128)S(1)}, f32[18,1,512]{2,1,0:T(1,128)S(1)}, u32[]{:S(2)}, u32[]{:S(2)}) collective-permute-start(f32[18,1,512]{2,1,0:T(1,128)S(1)} %get-tuple-element.86), channel_id=1, source_target_pairs={{1,0},{2,1},{3,2},{4,3},{5,4},{6,5},{7,6},{8,7},{9,8},{10,9},{11,1... | collective-permute-start | bytes 110600 | tf_op jit(solution)/shard_map/ppermute | solution.py:25
  375.3 1.9 collective-permute-start.18
  375.5 6.8 %collective-permute-start.19 = (f32[18,1,512]{2,1,0:T(1,128)S(1)}, f32[18,1,512]{2,1,0:T(1,128)S(1)}, u32[]{:S(2)}, u32[]{:S(2)}) collective-permute-start(f32[18,1,512]{2,1,0:T(1,128)S(1)} %get-tuple-element.91), channel_id=1, source_target_pairs={{0,1},{1,2},{2,3},{3,4},{4,5},{5,6},{6,7},{7,8},{8,9},{9,10},{10,1... | collective-permute-start | bytes 110600 | tf_op jit(solution)/shard_map/ppermute | solution.py:23
  460.2 3.8 collective-permute-start.20
  461.0 4.9 collective-permute-start.21
  466.0 2.0 collective-permute-start.22
  466.3 6.7 %collective-permute-start.23 = (f32[18,1,512]{2,1,0:T(1,128)S(1)}, f32[18,1,512]{2,1,0:T(1,128)S(1)}, u32[]{:S(2)}, u32[]{:S(2)}) collective-permute-start(f32[18,1,512]{2,1,0:T(1,128)S(1)} %get-tuple-element.89), channel_id=1, source_target_pairs={{0,1},{1,2},{2,3},{3,4},{4,5},{5,6},{6,7},{7,8},{8,9},{9,10},{10,1... | collective-permute-start | bytes 110600 | tf_op jit(solution)/shard_map/ppermute | solution.py:23
  474.4 15.5 %collective-permute-start.26 = (f32[2,16,1,512]{3,2,1,0:T(1,128)S(1)}, f32[2,16,1,512]{3,2,1,0:T(1,128)S(1)}, u32[]{:S(2)}, u32[]{:S(2)}) collective-permute-start(f32[2,16,1,512]{3,2,1,0:T(1,128)S(1)} %get-tuple-element.81), channel_id=1, source_target_pairs={{31,0},{0,1},{1,2},{2,3},{3,4},{4,5},{5,6},{6,7},{7,8},{8,9},{9,10... | collective-permute-start | bytes 196616 | tf_op jit(solution)/shard_map/ppermute | solution.py:35
  474.5 12.6 %collective-permute-start.24 = (f32[2,1,8,512]{3,2,0,1:T(8,128)S(1)}, f32[2,1,8,512]{3,2,0,1:T(8,128)S(1)}, u32[]{:S(2)}, u32[]{:S(2)}) collective-permute-start(f32[2,1,8,512]{3,2,0,1:T(8,128)S(1)} %get-tuple-element.83), channel_id=1, source_target_pairs={{224,0},{0,32},{32,64},{64,96},{96,128},{128,160},{160,192},{192,2... | collective-permute-start | bytes 98312 | tf_op jit(solution)/shard_map/ppermute | solution.py:35
  474.7 13.9 %collective-permute-start.25 = (f32[2,1,8,512]{3,2,0,1:T(8,128)S(1)}, f32[2,1,8,512]{3,2,0,1:T(8,128)S(1)}, u32[]{:S(2)}, u32[]{:S(2)}) collective-permute-start(f32[2,1,8,512]{3,2,0,1:T(8,128)S(1)} %get-tuple-element.82), channel_id=1, source_target_pairs={{32,0},{64,32},{96,64},{128,96},{160,128},{192,160},{224,192},{0,2... | collective-permute-start | bytes 98312 | tf_op jit(solution)/shard_map/ppermute | solution.py:35
  477.8 22.7 %collective-permute-start.27 = (f32[2,16,1,512]{3,2,1,0:T(1,128)S(1)}, f32[2,16,1,512]{3,2,1,0:T(1,128)S(1)}, u32[]{:S(2)}, u32[]{:S(2)}) collective-permute-start(f32[2,16,1,512]{3,2,1,0:T(1,128)S(1)} %get-tuple-element.80), channel_id=1, source_target_pairs={{1,0},{2,1},{3,2},{4,3},{5,4},{6,5},{7,6},{8,7},{9,8},{10,9},{11,1... | collective-permute-start | bytes 196616 | tf_op jit(solution)/shard_map/ppermute | solution.py:35
  (14 other events, 188.9 us)
where the time goes:
time: 528 us; the launch traced here: 518 us
  blocking collectives  364 us (69%)
  starting transfers between devices  44.8 us (8%)
  other arithmetic  38.5 us (7%)
  waiting for transfers between devices  35.6 us (7%)
  local copies, waits for them, and re-layouts  27.1 us (5%)
  between operations  8.26 us (2%)
    psum x3, blocking collectives, squares_sum(): return lax.psum(jnp.sum(residual * residual), ('gx', 'gy'))  219 us
    psum x2, blocking collectives, local(): step_size = norm_now / lax.psum(jnp.sum(direction * mapped), ('gx', 'gy'))  144 us
    ppermute x14, starting transfers between devices, padded_2(): lax.ppermute(head, axis, [((i + 1) % count, i) for i in range(count)])  31.7 us
    ppermute x14, waiting for transfers between devices, padded_2(): lax.ppermute(tail, axis, [(i, (i + 1) % count) for i in range(count)])  29.8 us
    unnamed x12, other arithmetic  11.6 us
  transfers between devices with their start and end apart: 32, of which 15 were waited for; matrix products, arithmetic and copies ran while one was open for 8% of the time, Pallas kernels for 0%

commit v1 on v0

v1 whole, which is shorter than its diff:
```python
import jax
import jax.numpy as jnp
from jax import lax
from jax.experimental import pallas as pl
from jax.experimental.pallas import tpu as pltpu
from jax.sharding import PartitionSpec as P

SCREEN_RATE = 0.01
WEIGHTS = (0.25, 0.125, 0.125, 0.125, 0.125, 0.125, 0.125)
OPPOSITE = (0, 2, 1, 4, 3, 6, 5)
DRIFT_COEF = (-0.02, 0.016)
RELAX_TIME = (0.8, 1.1)

H = 5
T = 8
SCALE = 0.0625

PREV, SIGMA, FLAGS, CHARGE = (0, 5), (5, 5), (10, 4), (14, 3)
DENS, POP, SOLID = 17, 19, 21
FACE_ROWS = 24

CORNER = (
    ("prev", 1, 4, 0, 0), ("prev", 2, 3, 0, 4), ("prev", 4, 1, 0, 7),
    ("sigma", 1, 4, 1, 0), ("sigma", 2, 3, 1, 4), ("sigma", 4, 1, 1, 7),
    ("prev", 3, 2, 2, 0), ("sigma", 3, 2, 2, 2), ("flags", 2, 2, 2, 4), ("charge", 2, 2, 2, 6),
    ("flags", 1, 3, 3, 0), ("charge", 1, 3, 3, 3), ("flags", 3, 1, 3, 6), ("charge", 3, 1, 3, 7),
)
SPAN = {"prev": PREV, "sigma": SIGMA, "flags": FLAGS, "charge": CHARGE}
VMEM = pl.BlockSpec(memory_space=pltpu.VMEM)
F32 = jnp.float32


def params(mib):
    return pltpu.CompilerParams(vmem_limit_bytes=mib * 1024 * 1024)


def pack_kernel(pops, cond, mask, flags, prev, charge, sigma, xlo, xhi, ylo, yhi):
    nx = cond.shape[0]

    def fields(x):
        d0 = pops[0, 0, x]
        d1 = pops[1, 0, x]
        for i in range(1, 7):
            d0 = d0 + pops[0, i, x]
            d1 = d1 + pops[1, i, x]
        solid = mask[x].astype(F32)
        return d0, d1, 2.0 * d0 - 2.0 * d1, cond[x] * (1.0 + 3.0 * solid), solid

    def row(x, _):
        d0, d1, ch, sg, solid = fields(x)
        charge[x] = ch
        sigma[x] = sg
        fl = flags[x].astype(F32)
        pv = prev[x]
        for out, up, way in ((ylo, False, 4), (yhi, True, 3)):
            def put(first, n, value, skip=0):
                at = T - n - skip if up else skip
                out[x, first:first + n] = value[at:at + n]
            put(*PREV, pv)
            put(*SIGMA, sg)
            put(*FLAGS, fl)
            put(*CHARGE, ch, 1)
            put(DENS, 1, d0)
            put(DENS + 1, 1, d1)
            put(POP, 1, pops[0, way, x])
            put(POP + 1, 1, pops[1, way, x])
            put(SOLID, 1, solid)
            put(SOLID + 1, 2, solid)
        return 0

    lax.fori_loop(0, nx, row, 0)
    for out, up, way in ((xlo, False, 2), (xhi, True, 1)):
        def start(n, skip=0):
            return nx - n - skip if up else skip
        n = PREV[1]
        out[PREV[0]:PREV[0] + n] = prev[start(n):start(n) + n]
        out[SIGMA[0]:SIGMA[0] + n] = sigma[start(n):start(n) + n]
        n = FLAGS[1]
        out[FLAGS[0]:FLAGS[0] + n] = flags[start(n):start(n) + n].astype(F32)
        n = CHARGE[1]
        out[CHARGE[0]:CHARGE[0] + n] = charge[start(n, 1):start(n, 1) + n]
        edge = start(1)
        d0, d1, _, _, solid = fields(edge)
        out[DENS] = d0
        out[DENS + 1] = d1
        out[POP] = pops[0, way, edge]
        out[POP + 1] = pops[1, way, edge]
        out[SOLID] = solid


def x_row(buf, side, name, distance):
    if name == "charge":
        if distance == 1:
            return 2.0 * buf[DENS] - 2.0 * buf[DENS + 1]
        return buf[CHARGE[0] + (4 - distance if side == 0 else distance - 2)]
    first, n = SPAN[name]
    return buf[first + (n - distance if side == 0 else distance - 1)]


def corner_kernel(xlo, xhi, clo, chi):
    for side, buf in ((0, xlo), (1, xhi)):
        for name, distance, n, tile, at in CORNER:
            value = x_row(buf, side, name, distance)
            clo[4 * side + tile, at:at + n] = value[:n]
            chi[4 * side + tile, at:at + n] = value[T - n:]


def harmonic(a, b):
    return 2.0 * a * b / (a + b)


def krylov_kernel(sigma, charge, flags, prev, xlo, xhi, ylo, yhi, clo, chi,
                  pv, v0, v1, v2, moments, sg, un, ch, wx, wy, wz):
    nx, _, nz = sigma.shape
    top = nx + H
    px = nx + 2 * H

    def own(x, _):
        at = x + H
        pv[at, T:2 * T] = prev[x]
        sg[at, T:2 * T] = sigma[x]
        un[at, T:2 * T] = 1.0 - flags[x].astype(F32)
        ch[at, T:2 * T] = charge[x]
        for buf, up in ((ylo, False), (yhi, True)):
            def put(ref, first, n, skip=0, one=False):
                to = 2 * T + skip if up else T - n - skip
                value = buf[x, first:first + n]
                ref[at, to:to + n] = 1.0 - value if one else value
            put(pv, *PREV)
            put(sg, *SIGMA)
            put(un, *FLAGS, 0, True)
            put(ch, *CHARGE, 1)
            to = 2 * T if up else T - 1
            ch[at, to:to + 1] = 2.0 * buf[x, DENS:DENS + 1] - 2.0 * buf[x, DENS + 1:DENS + 2]
        return 0

    lax.fori_loop(0, nx, own, 0)
    for side, buf in ((0, xlo), (1, xhi)):
        for distance in range(1, 6):
            at = H - distance if side == 0 else top - 1 + distance
            pv[at, T:2 * T] = x_row(buf, side, "prev", distance)
            sg[at, T:2 * T] = x_row(buf, side, "sigma", distance)
            if distance < 5:
                un[at, T:2 * T] = 1.0 - x_row(buf, side, "flags", distance)
                ch[at, T:2 * T] = x_row(buf, side, "charge", distance)
        for name, distance, n, tile, row in CORNER:
            at = H - distance if side == 0 else top - 1 + distance
            ref = {"prev": pv, "sigma": sg, "flags": un, "charge": ch}[name]
            for buf_y, to in ((clo, T - n), (chi, 2 * T)):
                value = buf_y[4 * side + tile, row:row + n]
                ref[at, to:to + n] = 1.0 - value if name == "flags" else value

    lane = lax.broadcasted_iota(jnp.int32, (3 * T, nz), 1)
    first, last = lane == 0, lane == nz - 1

    def faces(x, _):
        a = sg[x]
        wx[x] = harmonic(a, sg[jnp.minimum(x + 1, px - 1)])
        wy[x] = harmonic(a, pltpu.roll(a, 3 * T - 1, 0))
        wz[x] = harmonic(a, jnp.where(last, a, pltpu.roll(a, nz - 1, 1)))
        return 0

    lax.fori_loop(0, px, faces, 0)

    def flux_x(ref, x):
        return wx[x] * (ref[x] - ref[x + 1])

    def laplace(ref, x, below):
        m = ref[x]
        fx = wx[x] * (m - ref[x + 1])
        fy = wy[x] * (m - pltpu.roll(m, 3 * T - 1, 0))
        fz = wz[x] * (m - jnp.where(last, 0.0, pltpu.roll(m, nz - 1, 1)))
        s = fx - below
        s = s + (fy - pltpu.roll(fy, 1, 0))
        s = s + (fz + jnp.where(first, sg[x] * m, -pltpu.roll(fz, 1, 1)))
        return s + SCREEN_RATE * m, fx

    def sweep(src, lo, hi, store):
        def body(x, below):
            value, below = laplace(src, x, below)
            store(x, value)
            return below
        lax.fori_loop(lo, hi, body, flux_x(src, lo - 1))

    def store_v0(x, value):
        v0[x] = un[x] * (ch[x] - value)

    def apply_to(src, dst):
        def store(x, value):
            u = un[x]
            dst[x] = (u * value + (1.0 - u) * src[x]) * SCALE
        return store

    sweep(pv, H - 4, top + 4, store_v0)
    sweep(v0, H - 3, top + 3, apply_to(v0, v1))
    sweep(v1, H - 2, top + 2, apply_to(v1, v2))

    def last_sweep(x, carry):
        below, acc = carry
        value, below = laplace(v2, x, below)
        u = un[x, T:2 * T]
        a, b, c = v0[x, T:2 * T], v1[x, T:2 * T], v2[x, T:2 * T]
        d = (u * value[T:2 * T] + (1.0 - u) * c) * SCALE
        terms = (a * a, a * b, b * b, b * c, c * c, c * d)
        return below, tuple(s + t for s, t in zip(acc, terms))

    zero = jnp.zeros((T, nz), F32)
    _, acc = lax.fori_loop(H, top, last_sweep, (flux_x(v2, H - 1), (zero,) * 6))
    rows = moments.shape[0]
    col = lax.broadcasted_iota(jnp.int32, (rows, 128), 1)
    out = jnp.zeros((rows, 128), F32)
    for k, value in enumerate(acc):
        total = jnp.sum(jnp.sum(value, axis=0, keepdims=True), axis=1, keepdims=True)
        out = jnp.where(col == k, total, out)
    moments[...] = out


def cg_coefficients(mu):
    def form(p, shift):
        total = None
        for i, a in enumerate(p):
            for j, b in enumerate(p):
                term = a * b * mu[i + j + shift]
                total = term if total is None else total + term
        return total

    one = jnp.ones_like(mu[0])
    a0 = mu[0] / mu[1]
    r1 = (one, -a0)
    n1 = form(r1, 0)
    b0 = n1 / mu[0]
    p1 = (one + b0, -a0)
    a1 = n1 / form(p1, 1)
    r2 = (one, r1[1] - a1 * p1[0], -a1 * p1[1])
    n2 = form(r2, 0)
    b1 = n2 / n1
    p2 = (r2[0] + b1 * p1[0], r2[1] + b1 * p1[1], r2[2])
    a2 = n2 / form(p2, 1)
    return (a0 + a1 * p1[0] + a2 * p2[0], a1 * p1[1] + a2 * p2[1], a2 * p2[2])


def step_kernel(moments, pops, mask, pv, v0, v1, v2, xlo, xhi, ylo, yhi,
                potential, nxt, pot, coll):
    nx, _, nz = mask.shape
    top = nx + H
    row = jnp.sum(moments[...], axis=0, keepdims=True)
    col = lax.broadcasted_iota(jnp.int32, (1, 128), 1)
    mu = [jnp.sum(jnp.where(col == k, row, 0.0), axis=1, keepdims=True) for k in range(6)]
    coef = [c * SCALE for c in cg_coefficients(mu)]

    def correct(x, _):
        pot[x] = pv[x] + (coef[0] * v0[x] + coef[1] * v1[x] + coef[2] * v2[x])
        return 0

    lax.fori_loop(H - 2, top + 2, correct, 0)

    lane = lax.broadcasted_iota(jnp.int32, (T, nz), 1)
    line = lax.broadcasted_iota(jnp.int32, (T, nz), 0)

    def moved(species, way, current, density, grad):
        sign = 1.0 if way % 2 == 1 else -1.0
        velocity = sign * (DRIFT_COEF[species] * grad)
        balance = WEIGHTS[way] * density * (1.0 + 4.0 * velocity)
        return current - (1.0 / RELAX_TIME[species]) * (current - balance)

    for species in range(2):
        grad = 0.5 * (pot[H, T:2 * T] - pot[H - 2, T:2 * T])
        coll[species, 1, 0] = moved(species, 1, xlo[POP + species], xlo[DENS + species], grad)
        grad = 0.5 * (pot[top + 1, T:2 * T] - pot[top - 1, T:2 * T])
        coll[species, 2, nx + 1] = moved(species, 2, xhi[POP + species], xhi[DENS + species], grad)

    def collide(x, _):
        at = x + H
        wide = pot[at]
        mid = wide[T:2 * T]
        potential[x] = mid
        gx = 0.5 * (pot[at + 1, T:2 * T] - pot[at - 1, T:2 * T])
        gy = 0.5 * (pltpu.roll(wide, 3 * T - 1, 0)[T:2 * T] - pltpu.roll(wide, 1, 0)[T:2 * T])
        gz = 0.5 * (jnp.where(lane == nz - 1, 0.0, pltpu.roll(mid, nz - 1, 1))
                    - jnp.where(lane == 0, 0.0, pltpu.roll(mid, 1, 1)))
        grads = (None, gx, gx, gy, gy, gz, gz)
        for species in range(2):
            current = [pops[species, i, x] for i in range(7)]
            density = current[0]
            for i in range(1, 7):
                density = density + current[i]
            rate = 1.0 / RELAX_TIME[species]
            coll[species, 0, x + 1] = current[0] - rate * (current[0] - WEIGHTS[0] * density)
            for i in range(1, 7):
                coll[species, i, x + 1] = moved(species, i, current[i], density, grads[i])
        return 0

    lax.fori_loop(0, nx, collide, 0)

    def stream(x, _):
        at = x + H
        solid = mask[x].astype(F32)
        below = jnp.where(x == 0, xlo[SOLID], mask[jnp.maximum(x - 1, 0)].astype(F32))
        above = jnp.where(x == nx - 1, xhi[SOLID], mask[jnp.minimum(x + 1, nx - 1)].astype(F32))
        blocked = (
            None,
            below > 0.5,
            above > 0.5,
            jnp.where(line == 0, ylo[x, SOLID:SOLID + 1], pltpu.roll(solid, 1, 0)) > 0.5,
            jnp.where(line == T - 1, yhi[x, SOLID:SOLID + 1], pltpu.roll(solid, T - 1, 0)) > 0.5,
            jnp.where(lane == 0, 1.0, pltpu.roll(solid, 1, 1)) > 0.5,
            jnp.where(lane == nz - 1, 1.0, pltpu.roll(solid, nz - 1, 1)) > 0.5,
        )
        free = 1.0 - solid
        grad_lo = 0.5 * (pot[at, T:T + 1] - pot[at, T - 2:T - 1])
        grad_hi = 0.5 * (pot[at, 2 * T + 1:2 * T + 2] - pot[at, 2 * T - 1:2 * T])
        for species in range(2):
            c = [None] + [coll[species, i, x + 1] for i in range(1, 7)]
            from_lo = moved(species, 3, ylo[x, POP + species:POP + species + 1],
                            ylo[x, DENS + species:DENS + species + 1], grad_lo)
            from_hi = moved(species, 4, yhi[x, POP + species:POP + species + 1],
                            yhi[x, DENS + species:DENS + species + 1], grad_hi)
            source = (
                None,
                coll[species, 1, x],
                coll[species, 2, x + 2],
                jnp.where(line == 0, from_lo, pltpu.roll(c[3], 1, 0)),
                jnp.where(line == T - 1, from_hi, pltpu.roll(c[4], T - 1, 0)),
                pltpu.roll(c[5], 1, 1),
                pltpu.roll(c[6], nz - 1, 1),
            )
            nxt[species, 0, x] = coll[species, 0, x + 1] * free
            for i in range(1, 7):
                nxt[species, i, x] = jnp.where(blocked[i], c[OPPOSITE[i]], source[i]) * free
        return 0

    lax.fori_loop(0, nx, stream, 0)


def shift(block, axis, distance):
    n = lax.axis_size(axis)
    return lax.ppermute(block, axis, [(i, (i + distance) % n) for i in range(n)])


def local(populations, conductivity, deposit_mask, electrode_flags, previous_potential):
    nx, ny, nz = conductivity.shape
    brick = jax.ShapeDtypeStruct((nx, ny, nz), F32)
    x_face = jax.ShapeDtypeStruct((22, ny, nz), F32)
    y_face = jax.ShapeDtypeStruct((nx, FACE_ROWS, nz), F32)
    charge, sigma, xlo_s, xhi_s, ylo_s, yhi_s = pl.pallas_call(
        pack_kernel,
        out_shape=(brick, brick, x_face, x_face, y_face, y_face),
        in_specs=[VMEM] * 5,
        out_specs=(VMEM,) * 6,
        compiler_params=params(16),
        name="pack",
    )(populations, conductivity, deposit_mask, electrode_flags, previous_potential)
    xlo = shift(xhi_s, "gx", 1)
    xhi = shift(xlo_s, "gx", -1)
    ylo = shift(yhi_s, "gy", 1)
    yhi = shift(ylo_s, "gy", -1)
    corner = jax.ShapeDtypeStruct((8, ny, nz), F32)
    clo_s, chi_s = pl.pallas_call(
        corner_kernel,
        out_shape=(corner, corner),
        in_specs=[VMEM] * 2,
        out_specs=(VMEM,) * 2,
        compiler_params=params(8),
        name="corners",
    )(xlo, xhi)
    clo = shift(chi_s, "gy", 1)
    chi = shift(clo_s, "gy", -1)
    shape = (nx + 2 * H, 3 * T, nz)
    padded = jax.ShapeDtypeStruct(shape, F32)
    count = lax.axis_size("gx") * lax.axis_size("gy")
    pv, v0, v1, v2, moments = pl.pallas_call(
        krylov_kernel,
        out_shape=(padded,) * 4 + (jax.ShapeDtypeStruct((count, 128), F32),),
        in_specs=[VMEM] * 10,
        out_specs=(VMEM,) * 5,
        scratch_shapes=[pltpu.VMEM(shape, F32)] * 6,
        compiler_params=params(24),
        name="krylov",
    )(sigma, charge, electrode_flags, previous_potential, xlo, xhi, ylo, yhi, clo, chi)
    moments = lax.all_to_all(moments, ("gx", "gy"), 0, 0, tiled=True)
    return pl.pallas_call(
        step_kernel,
        out_shape=(brick, jax.ShapeDtypeStruct(populations.shape, F32)),
        in_specs=[VMEM] * 11,
        out_specs=(VMEM,) * 2,
        scratch_shapes=[
            pltpu.VMEM(shape, F32),
            pltpu.VMEM((2, 7, nx + 2, ny, nz), F32),
        ],
        compiler_params=params(28),
        name="step",
    )(moments, populations, deposit_mask, pv, v0, v1, v2, xlo, xhi, ylo, yhi)


def solution(mesh):
    in_specs = (
        P(None, None, "gx", "gy", None),
        P("gx", "gy", None),
        P("gx", "gy", None),
        P("gx", "gy", None),
        P("gx", "gy", None),
    )
    out_specs = (P("gx", "gy", None), P(None, None, "gx", "gy", None))
    return jax.shard_map(local, mesh=mesh, in_specs=in_specs, out_specs=out_specs, check_vma=False)
```

time: 528 us -> 79.7 us (0.15)
  the two profiles are of different devices: /device:TPU:0 before, /device:TPU:1 now
where the time goes in v1:
time: 79.7 us; the launch traced here: 79.5 us
  blocking collectives  26.8 us (34%)
  Pallas kernels  22.9 us (29%)
  starting transfers between devices  13.7 us (17%)
  waiting for transfers between devices  9.5 us (12%)
  local copies, waits for them, and re-layouts  5.85 us (7%)
    all_to_all x1, blocking collectives, local(): moments = lax.all_to_all(moments, ('gx', 'gy'), 0, 0, tiled=True)  26.8 us
    pallas_call x1, Pallas kernels, local(): pl.pallas_call(krylov_kernel, out_shape=(padded,) * 4 + (jax.ShapeDtypeSt...  16.7 us
    ppermute x6, starting transfers between devices, shift(): lax.ppermute(block, axis, [(i, (i + distance) % n) for i in range(n)])  13.7 us
    ppermute x6, waiting for transfers between devices, shift(): lax.ppermute(block, axis, [(i, (i + distance) % n) for i in range(n)])  9.5 us
    unnamed x18, local copies, waits for them, and re-layouts  5.85 us
    pallas_call x1, Pallas kernels, local(): pl.pallas_call(step_kernel, out_shape=(brick, jax.ShapeDtypeStruct(popula...  5.63 us
  transfers between devices with their start and end apart: 6, of which 3 were waited for; matrix products, arithmetic and copies ran while one was open for 0% of the time, Pallas kernels for 0%

profile of v1, /device:TPU:1, one launch (start us, length us, event | category | flops | bytes accessed | tf_op | source)
XLA Modules:
  0.0 79.5 jit_solution(9981409405588068892)
XLA Ops:
  0.6 0.0 copy-start
  0.6 2.0 %copy-done = f32[2,7,16,8,512]{4,3,2,1,0:T(8,128)S(1)} copy-done((f32[2,7,16,8,512]{4,3,2,1,0:T(8,128)S(1)}, f32[2,7,16,8,512]{4,3,2,1,0:T(8,128)}, u32[]{:S(2)}) %copy-start) | copy-done | bytes 3670040
  2.7 0.0 copy-start.2
  2.7 0.9 %copy-done.2 = s32[16,8,512]{2,1,0:T(8,128)S(1)} copy-done((s32[16,8,512]{2,1,0:T(8,128)S(1)}, s32[16,8,512]{2,1,0:T(8,128)}, u32[]{:S(2)}) %copy-start.2) | copy-done | bytes 262168
  3.6 0.0 copy-start.4
  3.6 0.9 %copy-done.4 = f32[16,8,512]{2,1,0:T(8,128)S(1)} copy-done((f32[16,8,512]{2,1,0:T(8,128)S(1)}, f32[16,8,512]{2,1,0:T(8,128)}, u32[]{:S(2)}) %copy-start.4) | copy-done | bytes 262168
  4.6 0.0 copy-start.6
  4.6 0.9 %copy-done.6 = s32[16,8,512]{2,1,0:T(8,128)S(1)} copy-done((s32[16,8,512]{2,1,0:T(8,128)S(1)}, s32[16,8,512]{2,1,0:T(8,128)}, u32[]{:S(2)}) %copy-start.6) | copy-done | bytes 262168
  5.5 0.0 copy-start.8
  5.5 0.9 %copy-done.8 = f32[16,8,512]{2,1,0:T(8,128)S(1)} copy-done((f32[16,8,512]{2,1,0:T(8,128)S(1)}, f32[16,8,512]{2,1,0:T(8,128)}, u32[]{:S(2)}) %copy-start.8) | copy-done | bytes 262168
  6.5 0.6 pack.1
  7.0 2.7 %collective-permute-start.2 = (f32[16,24,512]{2,1,0:T(8,128)S(1)}, f32[16,24,512]{2,1,0:T(8,128)S(1)}, u32[]{:S(2)}, u32[]{:S(2)}) collective-permute-start(f32[16,24,512]{2,1,0:T(8,128)S(1)} %get-tuple-element.19), channel_id=1, source_target_pairs={{0,1},{1,2},{2,3},{3,4},{4,5},{5,6},{6,7},{7,8},{8,9},{9,10},{10,1... | collective-permute-start | bytes 2359304 | tf_op jit(solution)/shard_map/ppermute | solution.py:337
  9.7 0.7 collective-permute-start.3
  10.5 0.9 %collective-permute-start = (f32[22,8,512]{2,1,0:T(8,128)S(1)}, f32[22,8,512]{2,1,0:T(8,128)S(1)}, u32[]{:S(2)}, u32[]{:S(2)}) collective-permute-start(f32[22,8,512]{2,1,0:T(8,128)S(1)} %get-tuple-element.17), channel_id=1, source_target_pairs={{0,32},{32,64},{64,96},{96,128},{128,160},{160,192},{192,224},{224... | collective-permute-start | bytes 1081352 | tf_op jit(solution)/shard_map/ppermute | solution.py:337
  11.4 3.9 %collective-permute-start.1 = (f32[22,8,512]{2,1,0:T(8,128)S(1)}, f32[22,8,512]{2,1,0:T(8,128)S(1)}, u32[]{:S(2)}, u32[]{:S(2)}) collective-permute-start(f32[22,8,512]{2,1,0:T(8,128)S(1)} %get-tuple-element.18), channel_id=1, source_target_pairs={{0,224},{32,0},{64,32},{96,64},{128,96},{160,128},{192,160},{224,1... | collective-permute-start | bytes 1081352 | tf_op jit(solution)/shard_map/ppermute | solution.py:337
  15.3 5.1 %collective-permute-done.xlo = f32[22,8,512]{2,1,0:T(8,128)S(1)} collective-permute-done((f32[22,8,512]{2,1,0:T(8,128)S(1)}, f32[22,8,512]{2,1,0:T(8,128)S(1)}, u32[]{:S(2)}, u32[]{:S(2)}) %collective-permute-start) | collective-permute-done | bytes 360480 | tf_op jit(solution)/shard_map/ppermute | solution.py:337
  20.4 0.0 collective-permute-done.1.xhi
  20.4 0.1 corners.1
  20.5 5.4 %collective-permute-start.4 = (f32[8,8,512]{2,1,0:T(8,128)S(1)}, f32[8,8,512]{2,1,0:T(8,128)S(1)}, u32[]{:S(2)}, u32[]{:S(2)}) collective-permute-start(f32[8,8,512]{2,1,0:T(8,128)S(1)} %get-tuple-element.21), channel_id=1, source_target_pairs={{0,1},{1,2},{2,3},{3,4},{4,5},{5,6},{6,7},{7,8},{8,9},{9,10},{10,1... | collective-permute-start | bytes 393224 | tf_op jit(solution)/shard_map/ppermute | solution.py:337
  25.9 0.0 collective-permute-start.5
  25.9 1.9 %collective-permute-done.4.clo = f32[8,8,512]{2,1,0:T(8,128)S(1)} collective-permute-done((f32[8,8,512]{2,1,0:T(8,128)S(1)}, f32[8,8,512]{2,1,0:T(8,128)S(1)}, u32[]{:S(2)}, u32[]{:S(2)}) %collective-permute-start.4) | collective-permute-done | bytes 131104 | tf_op jit(solution)/shard_map/ppermute | solution.py:337
  27.9 2.4 %collective-permute-done.5.chi = f32[8,8,512]{2,1,0:T(8,128)S(1)} collective-permute-done((f32[8,8,512]{2,1,0:T(8,128)S(1)}, f32[8,8,512]{2,1,0:T(8,128)S(1)}, u32[]{:S(2)}, u32[]{:S(2)}) %collective-permute-start.5) | collective-permute-done | bytes 131104 | tf_op jit(solution)/shard_map/ppermute | solution.py:337
  30.3 0.0 collective-permute-done.2.ylo
  30.3 0.0 collective-permute-done.3.yhi
  30.3 0.0 copy-done.3
  30.3 0.0 copy-done.5
  30.3 0.0 copy-start.1
  30.3 16.7 %krylov.1 = (f32[26,24,512]{2,1,0:T(8,128)S(1)}, f32[26,24,512]{2,1,0:T(8,128)S(1)}, f32[26,24,512]{2,1,0:T(8,128)S(1)}, f32[26,24,512]{2,1,0:T(8,128)S(1)}, f32[256,128]{1,0:T(8,128)S(1)}) custom-call(f32[16,8,512]{2,1,0:T(8,128)S(1)} %get-tuple-element.15.sigma, f32[16,8,512]{2,1,0:T(8,128)S(1)} %get-tuple-element.16.charge, s32[16,8,512]{2,1,0:T(8,128)S(1)} %copy-done.3, ...), custom_call_target="tpu_custom_call" | custom-call | tf_op jit(solution)/shard_map/krylov/pallas_call | solution.py:371
  47.0 26.8 %all_to_all.11 = f32[256,1,128]{2,1,0:T(1,128)S(1)} all-to-all(f32[256,1,128]{2,1,0:T(1,128)S(1)} %bitcast.5), channel_id=1, replica_groups=mesh['gx'=8,'gy'=32] {'gx','gy'}, dimensions={0} | all-to-all | bytes 262144 | tf_op jit(solution)/shard_map/all_to_all | solution.py:380
  73.8 0.0 copy-done.7
  73.8 0.0 copy-done.1
  73.8 5.6 %step.1 = (f32[16,8,512]{2,1,0:T(8,128)}, f32[2,7,16,8,512]{4,3,2,1,0:T(8,128)}) custom-call(f32[256,128]{1,0:T(8,128)S(1)} %bitcast.4, f32[2,7,16,8,512]{4,3,2,1,0:T(8,128)S(1)} %copy-done.1, s32[16,8,512]{2,1,0:T(8,128)S(1)} %copy-done.7, f32[26,24,512]{2,1,0:T(8,128)S(1)} %get-tuple-element.24.pv, f32[26,24,512]{2,1,0:T(8,128)S(1)} %get-tuple-element.25.v0, ...), custom_call_target="tpu_custom_call" | custom-call | tf_op jit(solution)/shard_map/step/pallas_call | solution.py:381
  (3 shorter events, 0.0 us)
Async XLA Ops:
  0.6 2.0 %copy-start = (f32[2,7,16,8,512]{4,3,2,1,0:T(8,128)S(1)}, f32[2,7,16,8,512]{4,3,2,1,0:T(8,128)}, u32[]{:S(2)}) copy-start(f32[2,7,16,8,512]{4,3,2,1,0:T(8,128)} %pops.3) | copy-start | bytes 11010052
  2.7 0.9 %copy-start.2 = (s32[16,8,512]{2,1,0:T(8,128)S(1)}, s32[16,8,512]{2,1,0:T(8,128)}, u32[]{:S(2)}) copy-start(s32[16,8,512]{2,1,0:T(8,128)} %flags.3) | copy-start | bytes 786436
  3.6 0.9 %copy-start.4 = (f32[16,8,512]{2,1,0:T(8,128)S(1)}, f32[16,8,512]{2,1,0:T(8,128)}, u32[]{:S(2)}) copy-start(f32[16,8,512]{2,1,0:T(8,128)} %prev.3) | copy-start | bytes 786436
  4.6 0.9 %copy-start.6 = (s32[16,8,512]{2,1,0:T(8,128)S(1)}, s32[16,8,512]{2,1,0:T(8,128)}, u32[]{:S(2)}) copy-start(s32[16,8,512]{2,1,0:T(8,128)} %mask.3) | copy-start | bytes 786436
  5.5 0.9 %copy-start.8 = (f32[16,8,512]{2,1,0:T(8,128)S(1)}, f32[16,8,512]{2,1,0:T(8,128)}, u32[]{:S(2)}) copy-start(f32[16,8,512]{2,1,0:T(8,128)} %cond.1) | copy-start | bytes 786436
  6.5 23.8 %copy-start.3 = (s32[16,8,512]{2,1,0:T(8,128)S(1)}, s32[16,8,512]{2,1,0:T(8,128)}, u32[]{:S(2)}) copy-start(s32[16,8,512]{2,1,0:T(8,128)} %flags.3) | copy-start | bytes 786436
  6.5 23.8 %copy-start.5 = (f32[16,8,512]{2,1,0:T(8,128)S(1)}, f32[16,8,512]{2,1,0:T(8,128)}, u32[]{:S(2)}) copy-start(f32[16,8,512]{2,1,0:T(8,128)} %prev.3) | copy-start | bytes 786436
  7.0 23.3 %collective-permute-start.2 = (f32[16,24,512]{2,1,0:T(8,128)S(1)}, f32[16,24,512]{2,1,0:T(8,128)S(1)}, u32[]{:S(2)}, u32[]{:S(2)}) collective-permute-start(f32[16,24,512]{2,1,0:T(8,128)S(1)} %get-tuple-element.19), channel_id=1, source_target_pairs={{0,1},{1,2},{2,3},{3,4},{4,5},{5,6},{6,7},{7,8},{8,9},{9,10},{10,1... | collective-permute-start | bytes 2359304 | tf_op jit(solution)/shard_map/ppermute | solution.py:337
  9.7 20.6 %collective-permute-start.3 = (f32[16,24,512]{2,1,0:T(8,128)S(1)}, f32[16,24,512]{2,1,0:T(8,128)S(1)}, u32[]{:S(2)}, u32[]{:S(2)}) collective-permute-start(f32[16,24,512]{2,1,0:T(8,128)S(1)} %get-tuple-element.20), channel_id=1, source_target_pairs={{0,31},{1,0},{2,1},{3,2},{4,3},{5,4},{6,5},{7,6},{8,7},{9,8},{10,9... | collective-permute-start | bytes 2359304 | tf_op jit(solution)/shard_map/ppermute | solution.py:337
  10.5 10.0 %collective-permute-start = (f32[22,8,512]{2,1,0:T(8,128)S(1)}, f32[22,8,512]{2,1,0:T(8,128)S(1)}, u32[]{:S(2)}, u32[]{:S(2)}) collective-permute-start(f32[22,8,512]{2,1,0:T(8,128)S(1)} %get-tuple-element.17), channel_id=1, source_target_pairs={{0,32},{32,64},{64,96},{96,128},{128,160},{160,192},{192,224},{224... | collective-permute-start | bytes 1081352 | tf_op jit(solution)/shard_map/ppermute | solution.py:337
  11.4 9.0 %collective-permute-start.1 = (f32[22,8,512]{2,1,0:T(8,128)S(1)}, f32[22,8,512]{2,1,0:T(8,128)S(1)}, u32[]{:S(2)}, u32[]{:S(2)}) collective-permute-start(f32[22,8,512]{2,1,0:T(8,128)S(1)} %get-tuple-element.18), channel_id=1, source_target_pairs={{0,224},{32,0},{64,32},{96,64},{128,96},{160,128},{192,160},{224,1... | collective-permute-start | bytes 1081352 | tf_op jit(solution)/shard_map/ppermute | solution.py:337
  20.4 53.4 %copy-start.7 = (s32[16,8,512]{2,1,0:T(8,128)S(1)}, s32[16,8,512]{2,1,0:T(8,128)}, u32[]{:S(2)}) copy-start(s32[16,8,512]{2,1,0:T(8,128)} %mask.3) | copy-start | bytes 786436
  20.5 7.4 %collective-permute-start.4 = (f32[8,8,512]{2,1,0:T(8,128)S(1)}, f32[8,8,512]{2,1,0:T(8,128)S(1)}, u32[]{:S(2)}, u32[]{:S(2)}) collective-permute-start(f32[8,8,512]{2,1,0:T(8,128)S(1)} %get-tuple-element.21), channel_id=1, source_target_pairs={{0,1},{1,2},{2,3},{3,4},{4,5},{5,6},{6,7},{7,8},{8,9},{9,10},{10,1... | collective-permute-start | bytes 393224 | tf_op jit(solution)/shard_map/ppermute | solution.py:337
  25.9 4.4 %collective-permute-start.5 = (f32[8,8,512]{2,1,0:T(8,128)S(1)}, f32[8,8,512]{2,1,0:T(8,128)S(1)}, u32[]{:S(2)}, u32[]{:S(2)}) collective-permute-start(f32[8,8,512]{2,1,0:T(8,128)S(1)} %get-tuple-element.22), channel_id=1, source_target_pairs={{0,31},{1,0},{2,1},{3,2},{4,3},{5,4},{6,5},{7,6},{8,7},{9,8},{10,9... | collective-permute-start | bytes 393224 | tf_op jit(solution)/shard_map/ppermute | solution.py:337
  30.3 43.5 %copy-start.1 = (f32[2,7,16,8,512]{4,3,2,1,0:T(8,128)S(1)}, f32[2,7,16,8,512]{4,3,2,1,0:T(8,128)}, u32[]{:S(2)}) copy-start(f32[2,7,16,8,512]{4,3,2,1,0:T(8,128)} %pops.3) | copy-start | bytes 11010052

commit v2 on v1

v2 whole, which is shorter than its diff:
```python
import jax
import jax.numpy as jnp
from jax import lax
from jax.experimental import pallas as pl
from jax.experimental.pallas import tpu as pltpu
from jax.sharding import PartitionSpec as P

SCREEN_RATE = 0.01
WEIGHTS = (0.25, 0.125, 0.125, 0.125, 0.125, 0.125, 0.125)
OPPOSITE = (0, 2, 1, 4, 3, 6, 5)
DRIFT_COEF = (-0.02, 0.016)
RELAX_TIME = (0.8, 1.1)

H = 5
T = 8
SCALE = 0.0625

PREV, SIGMA, FLAGS, CHARGE = (0, 5), (5, 5), (10, 4), (14, 3)
DENS, POP, SOLID = 17, 19, 21
FACE_ROWS = 24

CORNER = (
    ("prev", 1, 4, 0, 0), ("prev", 2, 3, 0, 4), ("prev", 4, 1, 0, 7),
    ("sigma", 1, 4, 1, 0), ("sigma", 2, 3, 1, 4), ("sigma", 4, 1, 1, 7),
    ("prev", 3, 2, 2, 0), ("sigma", 3, 2, 2, 2), ("flags", 2, 2, 2, 4), ("charge", 2, 2, 2, 6),
    ("flags", 1, 3, 3, 0), ("charge", 1, 3, 3, 3), ("flags", 3, 1, 3, 6), ("charge", 3, 1, 3, 7),
)
SPAN = {"prev": PREV, "sigma": SIGMA, "flags": FLAGS, "charge": CHARGE}
VMEM = pl.BlockSpec(memory_space=pltpu.VMEM)
HBM = pl.BlockSpec(memory_space=pltpu.HBM)
F32 = jnp.float32


def params(mib):
    return pltpu.CompilerParams(vmem_limit_bytes=mib * 1024 * 1024)


def load_kernel(pops_hbm, cond_hbm, mask_hbm, flags_hbm, prev_hbm,
                pops, sigma, solid, flags, prev, charge, xlo, xhi, cond, mask, marks, sem):
    nx = sigma.shape[0]
    quarter = nx // 4
    small = [
        pltpu.make_async_copy(src, dst, sem.at[4 + i])
        for i, (src, dst) in enumerate(
            ((cond_hbm, cond), (mask_hbm, mask), (flags_hbm, marks), (prev_hbm, prev))
        )
    ]
    large = [
        pltpu.make_async_copy(
            pops_hbm.at[:, :, pl.ds(q * quarter, quarter)],
            pops.at[:, :, pl.ds(q * quarter, quarter)],
            sem.at[q],
        )
        for q in range(4)
    ]
    for copy in small + large:
        copy.start()
    for copy in small:
        copy.wait()
    for x in range(nx):
        s = mask[x].astype(F32)
        solid[x] = s
        sigma[x] = cond[x] * (1.0 + 3.0 * s)
        flags[x] = marks[x].astype(F32)

    def density(species, x):
        d = pops[species, 0, x]
        for i in range(1, 7):
            d = d + pops[species, i, x]
        return d

    def edge(out, x, way):
        out[DENS] = density(0, x)
        out[DENS + 1] = density(1, x)
        out[POP] = pops[0, way, x]
        out[POP + 1] = pops[1, way, x]
        out[SOLID] = solid[x]

    for q in range(4):
        large[q].wait()
        for x in range(q * quarter, (q + 1) * quarter):
            charge[x] = 2.0 * density(0, x) - 2.0 * density(1, x)
    for out, up, way in ((xlo, False, 2), (xhi, True, 1)):
        def start(n, skip=0):
            return nx - n - skip if up else skip
        for src, (first, n), skip in ((prev, PREV, 0), (sigma, SIGMA, 0), (flags, FLAGS, 0), (charge, CHARGE, 1)):
            out[first:first + n] = src[start(n, skip):start(n, skip) + n]
        edge(out, start(1), way)


def on_parity(run):
    odd = lax.rem(lax.axis_index("gy"), 2)
    pl.when(odd == 0)(lambda: run(1, 0))
    pl.when(odd == 1)(lambda: run(0, 1))


def pack_kernel(pops, sigma, solid, flags, prev, charge, mate, other):
    on_parity(lambda lo, hi: pack_faces(
        pops, sigma, solid, flags, prev, charge, (mate, other)[lo], (mate, other)[hi]))


def pack_faces(pops, sigma, solid, flags, prev, charge, ylo, yhi):
    nx = sigma.shape[0]

    def row(x, _):
        d0, d1 = pops[0, 0, x], pops[1, 0, x]
        for i in range(1, 7):
            d0 = d0 + pops[0, i, x]
            d1 = d1 + pops[1, i, x]
        values = (prev[x], sigma[x], flags[x], charge[x])
        sd = solid[x]
        for out, up, way in ((ylo, False, 4), (yhi, True, 3)):
            def put(first, n, value, skip=0):
                at = T - n - skip if up else skip
                out[x, first:first + n] = value[at:at + n]
            for value, (first, n), skip in zip(values, (PREV, SIGMA, FLAGS, CHARGE), (0, 0, 0, 1)):
                put(first, n, value, skip)
            put(DENS, 1, d0)
            put(DENS + 1, 1, d1)
            put(POP, 1, pops[0, way, x])
            put(POP + 1, 1, pops[1, way, x])
            put(SOLID, 1, sd)
            put(SOLID + 1, 2, sd)
        return 0

    lax.fori_loop(0, nx, row, 0, unroll=4)


def x_row(buf, side, name, distance):
    if name == "charge":
        if distance == 1:
            return 2.0 * buf[DENS] - 2.0 * buf[DENS + 1]
        return buf[CHARGE[0] + (4 - distance if side == 0 else distance - 2)]
    first, n = SPAN[name]
    return buf[first + (n - distance if side == 0 else distance - 1)]


def corner_kernel(xlo, xhi, mate, other):
    on_parity(lambda lo, hi: pack_corners(xlo, xhi, (mate, other)[lo], (mate, other)[hi]))


def pack_corners(xlo, xhi, clo, chi):
    for side, buf in ((0, xlo), (1, xhi)):
        for name, distance, n, tile, at in CORNER:
            value = x_row(buf, side, name, distance)
            clo[4 * side + tile, at:at + n] = value[:n]
            chi[4 * side + tile, at:at + n] = value[T - n:]


def harmonic(a, b):
    return 2.0 * a * b / (a + b)


def laplace(m, above, below_flux, wx, wy, wz, sg, first, last):
    nz = m.shape[1]
    fx = wx * (m - above)
    fy = wy * (m - pltpu.roll(m, 3 * T - 1, 0))
    fz = wz * (m - jnp.where(last, 0.0, pltpu.roll(m, nz - 1, 1)))
    s = fx - below_flux
    s = s + (fy - pltpu.roll(fy, 1, 0))
    s = s + (fz + jnp.where(first, sg * m, -pltpu.roll(fz, 1, 1)))
    return s + SCREEN_RATE * m, fx


def mapped(u, value, v):
    return (u * value + (1.0 - u) * v) * SCALE


def ends(nz):
    lane = lax.broadcasted_iota(jnp.int32, (3 * T, nz), 1)
    return lane == 0, lane == nz - 1


def dots(a, b, c, d):
    return (a * a, a * b, b * b, b * c, c * c, c * d)


def place_faces(sigma, charge, flags, prev, ylo, yhi, pv, sg, un, ch, rest_lo, rest_hi):
    nx = sigma.shape[0]

    def own(x, _):
        at = x + H
        pv[at, T:2 * T] = prev[x]
        sg[at, T:2 * T] = sigma[x]
        un[at, T:2 * T] = 1.0 - flags[x]
        ch[at, T:2 * T] = charge[x]
        for buf, up, rest in ((ylo, False, rest_lo), (yhi, True, rest_hi)):
            rest[x] = buf[x, 2 * T:3 * T]
            def put(ref, first, n, skip=0, one=False):
                to = 2 * T + skip if up else T - n - skip
                value = buf[x, first:first + n]
                ref[at, to:to + n] = 1.0 - value if one else value
            put(pv, *PREV)
            put(sg, *SIGMA)
            put(un, *FLAGS, 0, True)
            put(ch, *CHARGE, 1)
            to = 2 * T if up else T - 1
            ch[at, to:to + 1] = 2.0 * buf[x, DENS:DENS + 1] - 2.0 * buf[x, DENS + 1:DENS + 2]
        return 0

    lax.fori_loop(0, nx, own, 0, unroll=4)


def inner_kernel(sigma, charge, flags, prev, mate, other,
                 pv, sg, un, wx, wy, wz, v0, v1, v2, ch, sums, rest_lo, rest_hi):
    nx, _, nz = sigma.shape
    top = nx + H
    first, last = ends(nz)
    on_parity(lambda lo, hi: place_faces(
        sigma, charge, flags, prev, (mate, other)[lo], (mate, other)[hi], pv, sg, un, ch, rest_lo, rest_hi))

    def faces(x, a):
        b = sg[jnp.minimum(x + 1, top - 1)]
        wx[x] = harmonic(a, b)
        wy[x] = harmonic(a, pltpu.roll(a, 3 * T - 1, 0))
        wz[x] = harmonic(a, jnp.where(last, a, pltpu.roll(a, nz - 1, 1)))
        return b

    lax.fori_loop(H, top, faces, sg[H], unroll=4)

    def sweep(src, lo, hi, store, unroll):
        def body(x, below):
            value, below = laplace(src[x], src[x + 1], below, wx[x], wy[x], wz[x], sg[x], first, last)
            store(x, value)
            return below
        lax.fori_loop(lo, hi, body, wx[lo - 1] * (src[lo - 1] - src[lo]), unroll=unroll)

    def store_v0(x, value):
        v0[x] = un[x] * (ch[x] - value)

    def apply_to(src, dst):
        def store(x, value):
            dst[x] = mapped(un[x], value, src[x])
        return store

    sweep(pv, H + 1, top - 1, store_v0, 7)
    sweep(v0, H + 2, top - 2, apply_to(v0, v1), 6)
    sweep(v1, H + 3, top - 3, apply_to(v1, v2), 5)

    def last_sweep(x, carry):
        below, acc = carry
        value, below = laplace(v2[x], v2[x + 1], below, wx[x], wy[x], wz[x], sg[x], first, last)
        a, b, c = v0[x, T:2 * T], v1[x, T:2 * T], v2[x, T:2 * T]
        d = mapped(un[x, T:2 * T], value[T:2 * T], c)
        return below, tuple(s + t for s, t in zip(acc, dots(a, b, c, d)))

    zero = jnp.zeros((T, nz), F32)
    below = wx[H + 3] * (v2[H + 3] - v2[H + 4])
    _, acc = lax.fori_loop(H + 4, top - 4, last_sweep, (below, (zero,) * 6), unroll=4)
    for k, value in enumerate(acc):
        sums[k] = value


def outer_kernel(pv_in, sg_in, un_in, wx_in, wy_in, wz_in, v0_in, v1_in, v2_in, ch_in, sums,
                 xlo, xhi, mate, other,
                 pv_out, v0_out, v1_out, v2_out, moments, sg_out, un_out, ch_out, wx_out, wy_out, wz_out):
    nx, nz = pv_in.shape[0] - 2 * H, pv_in.shape[2]
    top = nx + H
    first, last = ends(nz)

    def outer(x):
        return x if x < 8 else x - (nx + 2 * H - 16)

    class Rows:
        def __init__(self, inner, out, lo, hi):
            self.inner, self.out, self.lo, self.hi = inner, out, lo, hi

        def __getitem__(self, x):
            return self.inner[x] if self.lo <= x < self.hi else self.out[outer(x)]

        def own(self, x):
            if self.lo <= x < self.hi:
                return self.inner[x, T:2 * T]
            return self.out[outer(x), T:2 * T]

        def __setitem__(self, x, value):
            self.out[outer(x)] = value

    pv, sg, un = Rows(pv_in, pv_out, H, top), Rows(sg_in, sg_out, H, top), Rows(un_in, un_out, H, top)
    wx, wy, wz = Rows(wx_in, wx_out, H, top - 1), Rows(wy_in, wy_out, H, top), Rows(wz_in, wz_out, H, top)
    v0, v1, v2 = Rows(v0_in, v0_out, H + 1, top - 1), Rows(v1_in, v1_out, H + 2, top - 2), Rows(v2_in, v2_out, H + 3, top - 3)

    ch = Rows(ch_in, ch_out, H, top)

    def row_at(side, distance):
        return outer(H - distance if side == 0 else top - 1 + distance)

    for side, buf in ((0, xlo), (1, xhi)):
        for distance in range(1, 6):
            at = row_at(side, distance)
            pv_out[at, T:2 * T] = x_row(buf, side, "prev", distance)
            sg_out[at, T:2 * T] = x_row(buf, side, "sigma", distance)
            if distance < 5:
                un_out[at, T:2 * T] = 1.0 - x_row(buf, side, "flags", distance)
                ch_out[at, T:2 * T] = x_row(buf, side, "charge", distance)

    def place_corners(lo, hi):
        for side in range(2):
            for name, distance, n, tile, row in CORNER:
                ref = {"prev": pv_out, "sigma": sg_out, "flags": un_out, "charge": ch_out}[name]
                for buf, to in (((mate, other)[lo], T - n), ((mate, other)[hi], 2 * T)):
                    value = buf[4 * side + tile, row:row + n]
                    ref[row_at(side, distance), to:to + n] = 1.0 - value if name == "flags" else value

    on_parity(place_corners)
    low, high = range(0, H), range(top - 1, top + H)
    for x in (*low, *high):
        a = sg[x]
        if x < top + H - 1:
            wx[x] = harmonic(a, sg[x + 1])
        if 0 < x < top + H - 1 and x != top - 1:
            wy[x] = harmonic(a, pltpu.roll(a, 3 * T - 1, 0))
            wz[x] = harmonic(a, jnp.where(last, a, pltpu.roll(a, nz - 1, 1)))

    def sweep(src, margin, store):
        for lo, hi in ((1 + margin, H + 1 + margin), (top - 1 - margin, top + 4 - margin)):
            below = wx[lo - 1] * (src[lo - 1] - src[lo])
            for x in range(lo, hi):
                value, below = laplace(src[x], src[x + 1], below, wx[x], wy[x], wz[x], sg[x], first, last)
                store(x, value)

    def store_v0(x, value):
        v0[x] = un[x] * (ch[x] - value)

    def apply_to(src, dst):
        def store(x, value):
            dst[x] = mapped(un[x], value, src[x])
        return store

    sweep(pv, 0, store_v0)
    sweep(v0, 1, apply_to(v0, v1))
    sweep(v1, 2, apply_to(v1, v2))
    acc = [sums[k] for k in range(6)]
    for lo, hi in ((H, H + 4), (top - 4, top)):
        below = wx[lo - 1] * (v2[lo - 1] - v2[lo])
        for x in range(lo, hi):
            value, below = laplace(v2[x], v2[x + 1], below, wx[x], wy[x], wz[x], sg[x], first, last)
            c = v2.own(x)
            d = mapped(un.own(x), value[T:2 * T], c)
            for k, term in enumerate(dots(v0.own(x), v1.own(x), c, d)):
                acc[k] = acc[k] + term
    rows = moments.shape[0]
    col = lax.broadcasted_iota(jnp.int32, (1, 128), 1)
    line = jnp.zeros((1, 128), F32)
    for k, value in enumerate(acc):
        total = jnp.sum(jnp.sum(value, axis=0, keepdims=True), axis=1, keepdims=True)
        line = jnp.where(col == k, total, line)
    moments[...] = jnp.broadcast_to(line, (rows, 128))


def cg_coefficients(mu):
    def form(p, shift):
        total = None
        for i, a in enumerate(p):
            for j, b in enumerate(p):
                term = a * b * mu[i + j + shift]
                total = term if total is None else total + term
        return total

    one = jnp.ones_like(mu[0])
    a0 = mu[0] / mu[1]
    r1 = (one, -a0)
    n1 = form(r1, 0)
    b0 = n1 / mu[0]
    p1 = (one + b0, -a0)
    a1 = n1 / form(p1, 1)
    r2 = (one, r1[1] - a1 * p1[0], -a1 * p1[1])
    n2 = form(r2, 0)
    b1 = n2 / n1
    p2 = (r2[0] + b1 * p1[0], r2[1] + b1 * p1[1], r2[2])
    a2 = n2 / form(p2, 1)
    return (a0 + a1 * p1[0] + a2 * p2[0], a1 * p1[1] + a2 * p2[1], a2 * p2[2])


def step_kernel(moments, pops, solids, pv, v0, v1, v2, pv_x, v0_x, v1_x, v2_x, xlo, xhi, ylo, yhi,
                potential_hbm, nxt_hbm, pot, coll, nxt, potential, sem):
    nx, _, nz = solids.shape
    top = nx + H
    row = jnp.sum(moments[...], axis=0, keepdims=True)
    col = lax.broadcasted_iota(jnp.int32, (1, 128), 1)
    mu = [jnp.sum(jnp.where(col == k, row, 0.0), axis=1, keepdims=True) for k in range(6)]
    coef = [c * SCALE for c in cg_coefficients(mu)]

    def corrected(p, a, b, c):
        return p + (coef[0] * a + coef[1] * b + coef[2] * c)

    def correct(x, _):
        pot[x] = corrected(pv[x], v0[x], v1[x], v2[x])
        return 0

    lax.fori_loop(H + 3, top - 3, correct, 0, unroll=5)
    for x in (*range(H - 2, H + 3), *range(top - 3, top + 2)):
        depth = min(x - H, top - 1 - x)
        out = x if x < 8 else x - (nx + 2 * H - 16)
        pot[x] = corrected(
            pv[x] if depth >= 0 else pv_x[out],
            v0[x] if depth >= 1 else v0_x[out],
            v1[x] if depth >= 2 else v1_x[out],
            v2_x[out],
        )

    lane = lax.broadcasted_iota(jnp.int32, (T, nz), 1)
    line = lax.broadcasted_iota(jnp.int32, (T, nz), 0)

    def moved(species, way, current, density, grad):
        sign = 1.0 if way % 2 == 1 else -1.0
        velocity = sign * (DRIFT_COEF[species] * grad)
        balance = WEIGHTS[way] * density * (1.0 + 4.0 * velocity)
        return current - (1.0 / RELAX_TIME[species]) * (current - balance)

    for species in range(2):
        grad = 0.5 * (pot[H, T:2 * T] - pot[H - 2, T:2 * T])
        coll[species, 1, 0] = moved(species, 1, xlo[POP + species], xlo[DENS + species], grad)
        grad = 0.5 * (pot[top + 1, T:2 * T] - pot[top - 1, T:2 * T])
        coll[species, 2, nx + 1] = moved(species, 2, xhi[POP + species], xhi[DENS + species], grad)

    def collide(x):
        at = x + H
        wide = pot[at]
        mid = wide[T:2 * T]
        potential[x] = mid
        gx = 0.5 * (pot[at + 1, T:2 * T] - pot[at - 1, T:2 * T])
        gy = 0.5 * (pltpu.roll(wide, 3 * T - 1, 0)[T:2 * T] - pltpu.roll(wide, 1, 0)[T:2 * T])
        gz = 0.5 * (jnp.where(lane == nz - 1, 0.0, pltpu.roll(mid, nz - 1, 1))
                    - jnp.where(lane == 0, 0.0, pltpu.roll(mid, 1, 1)))
        grads = (None, gx, gx, gy, gy, gz, gz)
        for species in range(2):
            current = [pops[species, i, x] for i in range(7)]
            density = current[0]
            for i in range(1, 7):
                density = density + current[i]
            rate = 1.0 / RELAX_TIME[species]
            coll[species, 0, x + 1] = current[0] - rate * (current[0] - WEIGHTS[0] * density)
            for i in range(1, 7):
                coll[species, i, x + 1] = moved(species, i, current[i], density, grads[i])

    def stream(x):
        at = x + H
        solid = solids[x]
        below = jnp.where(x == 0, xlo[SOLID], solids[jnp.maximum(x - 1, 0)])
        above = jnp.where(x == nx - 1, xhi[SOLID], solids[jnp.minimum(x + 1, nx - 1)])
        blocked = (
            None,
            below > 0.5,
            above > 0.5,
            jnp.where(line == 0, ylo[x, SOLID - 2 * T:SOLID - 2 * T + 1], pltpu.roll(solid, 1, 0)) > 0.5,
            jnp.where(line == T - 1, yhi[x, SOLID - 2 * T:SOLID - 2 * T + 1], pltpu.roll(solid, T - 1, 0)) > 0.5,
            jnp.where(lane == 0, 1.0, pltpu.roll(solid, 1, 1)) > 0.5,
            jnp.where(lane == nz - 1, 1.0, pltpu.roll(solid, nz - 1, 1)) > 0.5,
        )
        free = 1.0 - solid
        grad_lo = 0.5 * (pot[at, T:T + 1] - pot[at, T - 2:T - 1])
        grad_hi = 0.5 * (pot[at, 2 * T + 1:2 * T + 2] - pot[at, 2 * T - 1:2 * T])
        for species in range(2):
            c = [None] + [coll[species, i, x + 1] for i in range(1, 7)]
            from_lo = moved(species, 3, ylo[x, POP - 2 * T + species:POP - 2 * T + species + 1],
                            ylo[x, DENS - 2 * T + species:DENS - 2 * T + species + 1], grad_lo)
            from_hi = moved(species, 4, yhi[x, POP - 2 * T + species:POP - 2 * T + species + 1],
                            yhi[x, DENS - 2 * T + species:DENS - 2 * T + species + 1], grad_hi)
            source = (
                None,
                coll[species, 1, x],
                coll[species, 2, x + 2],
                jnp.where(line == 0, from_lo, pltpu.roll(c[3], 1, 0)),
                jnp.where(line == T - 1, from_hi, pltpu.roll(c[4], T - 1, 0)),
                pltpu.roll(c[5], 1, 1),
                pltpu.roll(c[6], nz - 1, 1),
            )
            nxt[species, 0, x] = coll[species, 0, x + 1] * free
            for i in range(1, 7):
                nxt[species, i, x] = jnp.where(blocked[i], c[OPPOSITE[i]], source[i]) * free

    def both(x, _):
        collide(x + 1)
        stream(x)
        return 0

    collide(0)
    quarter = nx // 4
    copies = []
    for q in range(4):
        end = (q + 1) * quarter
        lax.fori_loop(q * quarter, min(end, nx - 1), both, 0)
        if end == nx:
            stream(nx - 1)
        rows = pl.ds(q * quarter, quarter)
        copies.append(pltpu.make_async_copy(nxt.at[:, :, rows], nxt_hbm.at[:, :, rows], sem.at[q]))
        copies[-1].start()
        if end == nx:
            copies.append(pltpu.make_async_copy(potential, potential_hbm, sem.at[4]))
            copies[-1].start()
    for copy in copies:
        copy.wait()


def to_mate(block):
    n = lax.axis_size("gy")
    return lax.ppermute(block, "gy", [(i, i ^ 1) for i in range(n)])


def to_other(block):
    n = lax.axis_size("gy")
    return lax.ppermute(block, "gy", [(i, (i + (1 if i % 2 else -1)) % n) for i in range(n)])


def shift(block, axis, distance):
    n = lax.axis_size(axis)
    return lax.ppermute(block, axis, [(i, (i + distance) % n) for i in range(n)])


def local(populations, conductivity, deposit_mask, electrode_flags, previous_potential):
    nx, ny, nz = conductivity.shape
    brick = jax.ShapeDtypeStruct((nx, ny, nz), F32)
    x_face = jax.ShapeDtypeStruct((22, ny, nz), F32)
    y_face = jax.ShapeDtypeStruct((nx, FACE_ROWS, nz), F32)
    whole = jax.ShapeDtypeStruct(populations.shape, F32)
    pops, sigma, solid, flags, prev, charge, xlo_s, xhi_s = pl.pallas_call(
        load_kernel,
        out_shape=(whole, brick, brick, brick, brick, brick, x_face, x_face),
        in_specs=[HBM] * 5,
        out_specs=(VMEM,) * 8,
        scratch_shapes=[
            pltpu.VMEM(conductivity.shape, F32),
            pltpu.VMEM(conductivity.shape, jnp.int32),
            pltpu.VMEM(conductivity.shape, jnp.int32),
            pltpu.SemaphoreType.DMA((8,)),
        ],
        compiler_params=params(16),
        name="load",
    )(*(pltpu.with_memory_space_constraint(a, pltpu.HBM) for a in (
        populations, conductivity, deposit_mask, electrode_flags, previous_potential)))
    xlo = shift(xhi_s, "gx", 1)
    xhi = shift(xlo_s, "gx", -1)
    y_mate, y_other = pl.pallas_call(
        pack_kernel,
        out_shape=(y_face, y_face),
        in_specs=[VMEM] * 6,
        out_specs=(VMEM,) * 2,
        compiler_params=params(16),
        name="pack",
    )(pops, sigma, solid, flags, prev, charge)
    y_mate = to_mate(y_mate)
    y_other = to_other(y_other)
    corner = jax.ShapeDtypeStruct((8, ny, nz), F32)
    c_mate, c_other = pl.pallas_call(
        corner_kernel,
        out_shape=(corner, corner),
        in_specs=[VMEM] * 2,
        out_specs=(VMEM,) * 2,
        compiler_params=params(8),
        name="corners",
    )(xlo, xhi)
    c_mate = to_mate(c_mate)
    c_other = to_other(c_other)
    shape = (nx + 2 * H, 3 * T, nz)
    padded = jax.ShapeDtypeStruct(shape, F32)
    *inner, rest_lo, rest_hi = pl.pallas_call(
        inner_kernel,
        out_shape=(padded,) * 10 + (jax.ShapeDtypeStruct((6, ny, nz), F32), brick, brick),
        in_specs=[VMEM] * 6,
        out_specs=(VMEM,) * 13,
        compiler_params=params(24),
        cost_estimate=pl.CostEstimate(flops=60_000_000, bytes_accessed=20_000_000, transcendentals=0),
        name="inner",
    )(sigma, charge, flags, prev, y_mate, y_other)
    outer_shape = (16, 3 * T, nz)
    edges = jax.ShapeDtypeStruct(outer_shape, F32)
    count = lax.axis_size("gx") * lax.axis_size("gy")
    pv_x, v0_x, v1_x, v2_x, moments = pl.pallas_call(
        outer_kernel,
        out_shape=(edges,) * 4 + (jax.ShapeDtypeStruct((count, 128), F32),),
        in_specs=[VMEM] * 15,
        out_specs=(VMEM,) * 5,
        scratch_shapes=[pltpu.VMEM(outer_shape, F32)] * 6,
        compiler_params=params(28),
        name="outer",
    )(*inner, xlo, xhi, c_mate, c_other)
    moments = lax.all_to_all(moments, ("gx", "gy"), 0, 0, tiled=True)
    pv, v0, v1, v2 = (inner[i] for i in (0, 6, 7, 8))
    return pl.pallas_call(
        step_kernel,
        out_shape=(brick, whole),
        in_specs=[VMEM] * 15,
        out_specs=(HBM,) * 2,
        scratch_shapes=[
            pltpu.VMEM(shape, F32),
            pltpu.VMEM((2, 7, nx + 2, ny, nz), F32),
            pltpu.VMEM(populations.shape, F32),
            pltpu.VMEM(conductivity.shape, F32),
            pltpu.SemaphoreType.DMA((5,)),
        ],
        compiler_params=params(28),
        name="step",
    )(moments, pops, solid, pv, v0, v1, v2, pv_x, v0_x, v1_x, v2_x, xlo, xhi, rest_lo, rest_hi)


def solution(mesh):
    in_specs = (
        P(None, None, "gx", "gy", None),
        P("gx", "gy", None),
        P("gx", "gy", None),
        P("gx", "gy", None),
        P("gx", "gy", None),
    )
    out_specs = (P("gx", "gy", None), P(None, None, "gx", "gy", None))
    return jax.shard_map(local, mesh=mesh, in_specs=in_specs, out_specs=out_specs, check_vma=False)
```

time: 79.7 us -> 58.4 us (0.73)
  Pallas kernels: 22.9 us -> 12.8 us
  local copies, waits for them, and re-layouts: 5.85 us -> 0 us
  waiting for transfers between devices: 9.5 us -> 5.86 us
  blocking collectives: 26.8 us -> 25.7 us
    pallas_call x3 -> x5, Pallas kernels: 22.9 us -> 12.8 us  [the longest x1 3.5 us: local(): pl.pallas_call(inner_kernel, out_shape=(padded,) * 10 + (jax.ShapeDtypeSt...]
    ppermute x6 -> x2, starting transfers between devices: 13.7 us -> 5.04 us  [shift(): lax.ppermute(block, axis, [(i, (i + distance) % n) for i in range(n)])]
    ppermute x0 -> x4, starting transfers between devices: none -> 8.24 us  [the longest x2 8.12 us: to_mate(): return lax.ppermute(block, 'gy', [(i, i ^ 1) for i in range(n)])]
    unnamed x18 -> x0, local copies, waits for them, and re-layouts: 5.85 us -> none
    ppermute x6 -> x2, waiting for transfers between devices: 9.5 us -> 5.11 us  [shift(): lax.ppermute(block, axis, [(i, (i + distance) % n) for i in range(n)])]
    all_to_all x1, blocking collectives: 26.8 us -> 25.7 us  [local(): moments = lax.all_to_all(moments, ('gx', 'gy'), 0, 0, tiled=True)]
  transfers between devices with their start and end apart: 6 -> 6, of which waited for: 3 -> 2; matrix products, arithmetic and copies ran while one was open for 0% -> 0% of each run, Pallas kernels for 0% -> 6%
where the time goes in v2:
time: 58.4 us; the launch traced here: 58.3 us
  blocking collectives  25.7 us (44%)
  starting transfers between devices  13.3 us (23%)
  Pallas kernels  12.8 us (22%)
  waiting for transfers between devices  5.86 us (10%)
  between operations  0.68 us (1%)
    all_to_all x1, blocking collectives, local(): moments = lax.all_to_all(moments, ('gx', 'gy'), 0, 0, tiled=True)  25.7 us
    ppermute x2, starting transfers between devices, to_mate(): return lax.ppermute(block, 'gy', [(i, i ^ 1) for i in range(n)])  8.12 us
    ppermute x2, waiting for transfers between devices, shift(): lax.ppermute(block, axis, [(i, (i + distance) % n) for i in range(n)])  5.11 us
    ppermute x2, starting transfers between devices, shift(): lax.ppermute(block, axis, [(i, (i + distance) % n) for i in range(n)])  5.04 us
    pallas_call x1, Pallas kernels, local(): pl.pallas_call(inner_kernel, out_shape=(padded,) * 10 + (jax.ShapeDtypeSt...  3.5 us
    pallas_call x1, Pallas kernels, local(): pl.pallas_call(step_kernel, out_shape=(brick, whole), in_specs=[VMEM] * 1...  3.34 us
    pallas_call x1, Pallas kernels, local(): pl.pallas_call(outer_kernel, out_shape=(edges,) * 4 + (jax.ShapeDtypeStru...  2.96 us
    pallas_call x1, Pallas kernels, local(): pl.pallas_call(load_kernel, out_shape=(whole, brick, brick, brick, brick,...  2.5 us
  transfers between devices with their start and end apart: 6, of which 2 were waited for; matrix products, arithmetic and copies ran while one was open for 0% of the time, Pallas kernels for 6%

profile of v2, /device:TPU:1, one launch (start us, length us, event | category | flops | bytes accessed | tf_op | source)
XLA Modules:
  0.0 58.3 jit_solution(8593641847248330862)
XLA Ops:
  0.6 2.5 %load.1 = (f32[2,7,16,8,512]{4,3,2,1,0:T(8,128)S(1)}, f32[16,8,512]{2,1,0:T(8,128)S(1)}, f32[16,8,512]{2,1,0:T(8,128)S(1)}, f32[16,8,512]{2,1,0:T(8,128)S(1)}, f...) custom-call(f32[2,7,16,8,512]{4,3,2,1,0:T(8,128)} %pops_hbm.1, ...), custom_call_target="tpu_custom_call" | custom-call | tf_op jit(solution)/shard_map/load/pallas_call | solution.py:517
  3.1 0.5 pack.1
  3.6 3.3 %collective-permute-start = (f32[16,24,512]{2,1,0:T(8,128)S(1)}, f32[16,24,512]{2,1,0:T(8,128)S(1)}, u32[]{:S(2)}, u32[]{:S(2)}) collective-permute-start(f32[16,24,512]{2,1,0:T(8,128)S(1)} %get-tuple-element.38), channel_id=1, source_target_pairs={{0,1},{1,0},{2,3},{3,2},{4,5},{5,4},{6,7},{7,6},{8,9},{9,8},{10,11... | collective-permute-start | bytes 2359304 | tf_op jit(solution)/shard_map/ppermute | solution.py:498
  6.9 0.0 collective-permute-start.1
  6.9 1.1 %collective-permute-start.2 = (f32[22,8,512]{2,1,0:T(8,128)S(1)}, f32[22,8,512]{2,1,0:T(8,128)S(1)}, u32[]{:S(2)}, u32[]{:S(2)}) collective-permute-start(f32[22,8,512]{2,1,0:T(8,128)S(1)} %get-tuple-element.51), channel_id=1, source_target_pairs={{0,32},{32,64},{64,96},{96,128},{128,160},{160,192},{192,224},{224... | collective-permute-start | bytes 1081352 | tf_op jit(solution)/shard_map/ppermute | solution.py:508
  8.0 3.9 %collective-permute-start.3 = (f32[22,8,512]{2,1,0:T(8,128)S(1)}, f32[22,8,512]{2,1,0:T(8,128)S(1)}, u32[]{:S(2)}, u32[]{:S(2)}) collective-permute-start(f32[22,8,512]{2,1,0:T(8,128)S(1)} %get-tuple-element.52), channel_id=1, source_target_pairs={{0,224},{32,0},{64,32},{96,64},{128,96},{160,128},{192,160},{224,1... | collective-permute-start | bytes 1081352 | tf_op jit(solution)/shard_map/ppermute | solution.py:508
  12.0 5.1 %collective-permute-done.2.xlo = f32[22,8,512]{2,1,0:T(8,128)S(1)} collective-permute-done((f32[22,8,512]{2,1,0:T(8,128)S(1)}, f32[22,8,512]{2,1,0:T(8,128)S(1)}, u32[]{:S(2)}, u32[]{:S(2)}) %collective-permute-start.2) | collective-permute-done | bytes 360480 | tf_op jit(solution)/shard_map/ppermute | solution.py:508
  17.1 0.0 collective-permute-done.3.xhi
  17.1 0.1 corners.1
  17.1 4.8 %collective-permute-start.4 = (f32[8,8,512]{2,1,0:T(8,128)S(1)}, f32[8,8,512]{2,1,0:T(8,128)S(1)}, u32[]{:S(2)}, u32[]{:S(2)}) collective-permute-start(f32[8,8,512]{2,1,0:T(8,128)S(1)} %get-tuple-element.53), channel_id=1, source_target_pairs={{0,1},{1,0},{2,3},{3,2},{4,5},{5,4},{6,7},{7,6},{8,9},{9,8},{10,11... | collective-permute-start | bytes 393224 | tf_op jit(solution)/shard_map/ppermute | solution.py:498
  21.9 0.1 collective-permute-start.5
  22.1 0.0 collective-permute-done.mate
  22.1 0.0 collective-permute-done.1.other
  22.1 3.5 %inner.1 = (f32[26,24,512]{2,1,0:T(8,128)S(1)}, f32[26,24,512]{2,1,0:T(8,128)S(1)}, f32[26,24,512]{2,1,0:T(8,128)S(1)}, f32[26,24,512]{2,1,0:T(8,128)S(1)}, f32[...) custom-call(f32[16,8,512]{2,1,0:T(8,128)S(1)} %get-tuple-element.32., ...), custom_call_target="tpu_custom_call" | custom-call | flops 60000000 | bytes 20000000 | tf_op jit(solution)/shard_map/inner/pallas_call | solution.py:557
  25.6 0.0 collective-permute-done.4.mate
  25.6 0.7 %collective-permute-done.5.other = f32[8,8,512]{2,1,0:T(8,128)S(1)} collective-permute-done((f32[8,8,512]{2,1,0:T(8,128)S(1)}, f32[8,8,512]{2,1,0:T(8,128)S(1)}, u32[]{:S(2)}, u32[]{:S(2)}) %collective-permute-start.5) | collective-permute-done | bytes 131104 | tf_op jit(solution)/shard_map/ppermute | solution.py:503
  26.3 3.0 %outer.1 = (f32[16,24,512]{2,1,0:T(8,128)S(1)}, f32[16,24,512]{2,1,0:T(8,128)S(1)}, f32[16,24,512]{2,1,0:T(8,128)S(1)}, f32[16,24,512]{2,1,0:T(8,128)S(1)}, f32[256,128]{1,0:T(8,128)S(1)}) custom-call(f32[26,24,512]{2,1,0:T(8,128)S(1)} %get-tuple-element.40.pv_in.pv, f32[26,24,512]{2,1,0:T(8,128)S(1)} %get-tuple-element.41.sg_in, ...), custom_call_target="tpu_custom_call" | custom-call | tf_op jit(solution)/shard_map/outer/pallas_call | solution.py:569
  29.3 25.7 %all_to_all.11 = f32[256,1,128]{2,1,0:T(1,128)S(1)} all-to-all(f32[256,1,128]{2,1,0:T(1,128)S(1)} %bitcast.5), channel_id=1, replica_groups=mesh['gx'=8,'gy'=32] {'gx','gy'}, dimensions={0} | all-to-all | bytes 262144 | tf_op jit(solution)/shard_map/all_to_all | solution.py:578
  55.0 3.3 %step.1 = (f32[16,8,512]{2,1,0:T(8,128)}, f32[2,7,16,8,512]{4,3,2,1,0:T(8,128)}) custom-call(f32[256,128]{1,0:T(8,128)S(1)} %bitcast.4, f32[2,7,16,8,512]{4,3,2,1,0:T(8,128)S(1)} %get-tuple-element.36.pops, f32[16,8,512]{2,1,0:T(8,128)S(1)} %get-tuple-element.37.solid.solids, f32[26,24,512]{2,1,0:T(8,128)S(1)} %get-tuple-element.40.pv_in.pv, ...), custom_call_target="tpu_custom_call" | custom-call | tf_op jit(solution)/shard_map/step/pallas_call | solution.py:580
Async XLA Ops:
  3.6 18.5 %collective-permute-start = (f32[16,24,512]{2,1,0:T(8,128)S(1)}, f32[16,24,512]{2,1,0:T(8,128)S(1)}, u32[]{:S(2)}, u32[]{:S(2)}) collective-permute-start(f32[16,24,512]{2,1,0:T(8,128)S(1)} %get-tuple-element.38), channel_id=1, source_target_pairs={{0,1},{1,0},{2,3},{3,2},{4,5},{5,4},{6,7},{7,6},{8,9},{9,8},{10,11... | collective-permute-start | bytes 2359304 | tf_op jit(solution)/shard_map/ppermute | solution.py:498
  6.9 15.1 %collective-permute-start.1 = (f32[16,24,512]{2,1,0:T(8,128)S(1)}, f32[16,24,512]{2,1,0:T(8,128)S(1)}, u32[]{:S(2)}, u32[]{:S(2)}) collective-permute-start(f32[16,24,512]{2,1,0:T(8,128)S(1)} %get-tuple-element.39), channel_id=1, source_target_pairs={{0,31},{1,2},{2,1},{3,4},{4,3},{5,6},{6,5},{7,8},{8,7},{9,10},{10,... | collective-permute-start | bytes 2359304 | tf_op jit(solution)/shard_map/ppermute | solution.py:503
  6.9 10.1 %collective-permute-start.2 = (f32[22,8,512]{2,1,0:T(8,128)S(1)}, f32[22,8,512]{2,1,0:T(8,128)S(1)}, u32[]{:S(2)}, u32[]{:S(2)}) collective-permute-start(f32[22,8,512]{2,1,0:T(8,128)S(1)} %get-tuple-element.51), channel_id=1, source_target_pairs={{0,32},{32,64},{64,96},{96,128},{128,160},{160,192},{192,224},{224... | collective-permute-start | bytes 1081352 | tf_op jit(solution)/shard_map/ppermute | solution.py:508
  8.0 9.0 %collective-permute-start.3 = (f32[22,8,512]{2,1,0:T(8,128)S(1)}, f32[22,8,512]{2,1,0:T(8,128)S(1)}, u32[]{:S(2)}, u32[]{:S(2)}) collective-permute-start(f32[22,8,512]{2,1,0:T(8,128)S(1)} %get-tuple-element.52), channel_id=1, source_target_pairs={{0,224},{32,0},{64,32},{96,64},{128,96},{160,128},{192,160},{224,1... | collective-permute-start | bytes 1081352 | tf_op jit(solution)/shard_map/ppermute | solution.py:508
  17.1 8.4 %collective-permute-start.4 = (f32[8,8,512]{2,1,0:T(8,128)S(1)}, f32[8,8,512]{2,1,0:T(8,128)S(1)}, u32[]{:S(2)}, u32[]{:S(2)}) collective-permute-start(f32[8,8,512]{2,1,0:T(8,128)S(1)} %get-tuple-element.53), channel_id=1, source_target_pairs={{0,1},{1,0},{2,3},{3,2},{4,5},{5,4},{6,7},{7,6},{8,9},{9,8},{10,11... | collective-permute-start | bytes 393224 | tf_op jit(solution)/shard_map/ppermute | solution.py:498
  21.9 4.4 %collective-permute-start.5 = (f32[8,8,512]{2,1,0:T(8,128)S(1)}, f32[8,8,512]{2,1,0:T(8,128)S(1)}, u32[]{:S(2)}, u32[]{:S(2)}) collective-permute-start(f32[8,8,512]{2,1,0:T(8,128)S(1)} %get-tuple-element.54), channel_id=1, source_target_pairs={{0,31},{1,2},{2,1},{3,4},{4,3},{5,6},{6,5},{7,8},{8,7},{9,10},{10,... | collective-permute-start | bytes 393224 | tf_op jit(solution)/shard_map/ppermute | solution.py:503

commit v3 on v2

--- a/solution.py
+++ b/solution.py
@@ -35,8 +35,21 @@
     return pltpu.CompilerParams(vmem_limit_bytes=mib * 1024 * 1024)
 
 
+def density(pops, species, x):
+    d = pops[species, 0, x]
+    for i in range(1, 7):
+        d = d + pops[species, i, x]
+    return d
+
+
+def on_parity(run):
+    odd = lax.rem(lax.axis_index("gy"), 2)
+    pl.when(odd == 0)(lambda: run(1, 0))
+    pl.when(odd == 1)(lambda: run(0, 1))
+
+
 def load_kernel(pops_hbm, cond_hbm, mask_hbm, flags_hbm, prev_hbm,
-                pops, sigma, solid, flags, prev, charge, xlo, xhi, cond, mask, marks, sem):
+                pops, sigma, solid, flags, prev, charge, xlo, xhi, mate, other, cond, mask, marks, sem):
     nx = sigma.shape[0]
     quarter = nx // 4
     small = [
@@ -62,68 +75,98 @@
         solid[x] = s
         sigma[x] = cond[x] * (1.0 + 3.0 * s)
         flags[x] = marks[x].astype(F32)
-
-    def density(species, x):
-        d = pops[species, 0, x]
-        for i in range(1, 7):
-            d = d + pops[species, i, x]
-        return d
-
-    def edge(out, x, way):
-        out[DENS] = density(0, x)
-        out[DENS + 1] = density(1, x)
-        out[POP] = pops[0, way, x]
-        out[POP + 1] = pops[1, way, x]
-        out[SOLID] = solid[x]
-
+    for out, up in ((xlo, False), (xhi, True)):
+        for src, (first, n) in ((prev, PREV), (sigma, SIGMA), (flags, FLAGS)):
+            at = nx - n if up else 0
+            out[first:first + n] = src[at:at + n]
     for q in range(4):
         large[q].wait()
-        for x in range(q * quarter, (q + 1) * quarter):
-            charge[x] = 2.0 * density(0, x) - 2.0 * density(1, x)
-    for out, up, way in ((xlo, False, 2), (xhi, True, 1)):
-        def start(n, skip=0):
-            return nx - n - skip if up else skip
-        for src, (first, n), skip in ((prev, PREV, 0), (sigma, SIGMA, 0), (flags, FLAGS, 0), (charge, CHARGE, 1)):
-            out[first:first + n] = src[start(n, skip):start(n, skip) + n]
-        edge(out, start(1), way)
-
-
-def on_parity(run):
-    odd = lax.rem(lax.axis_index("gy"), 2)
-    pl.when(odd == 0)(lambda: run(1, 0))
-    pl.when(odd == 1)(lambda: run(0, 1))
-
-
-def pack_kernel(pops, sigma, solid, flags, prev, charge, mate, other):
-    on_parity(lambda lo, hi: pack_faces(
-        pops, sigma, solid, flags, prev, charge, (mate, other)[lo], (mate, other)[hi]))
-
-
-def pack_faces(pops, sigma, solid, flags, prev, charge, ylo, yhi):
-    nx = sigma.shape[0]
-
-    def row(x, _):
-        d0, d1 = pops[0, 0, x], pops[1, 0, x]
-        for i in range(1, 7):
-            d0 = d0 + pops[0, i, x]
-            d1 = d1 + pops[1, i, x]
-        values = (prev[x], sigma[x], flags[x], charge[x])
-        sd = solid[x]
+        rows = range(q * quarter, (q + 1) * quarter)
+        on_parity(lambda lo, hi: pack_faces(
+            pops, sigma, solid, flags, prev, charge, (mate, other)[lo], (mate, other)[hi], rows))
+        if q in (0, 3):
+            out, up, way = (xlo, False, 2) if q == 0 else (xhi, True, 1)
+            first, n = CHARGE
+            at = nx - n - 1 if up else 1
+            out[first:first + n] = charge[at:at + n]
+            edge = nx - 1 if up else 0
+            for species in range(2):
+                out[DENS + species] = density(pops, species, edge)
+                out[POP + species] = pops[species, way, edge]
+            out[SOLID] = solid[edge]
+
+
+def pack_faces(pops, sigma, solid, flags, prev, charge, ylo, yhi, rows):
+    for x in rows:
+        d = (density(pops, 0, x), density(pops, 1, x))
+        ch = 2.0 * d[0] - 2.0 * d[1]
+        charge[x] = ch
+        values = (prev[x], sigma[x], flags[x], ch)
         for out, up, way in ((ylo, False, 4), (yhi, True, 3)):
             def put(first, n, value, skip=0):
                 at = T - n - skip if up else skip
                 out[x, first:first + n] = value[at:at + n]
             for value, (first, n), skip in zip(values, (PREV, SIGMA, FLAGS, CHARGE), (0, 0, 0, 1)):
                 put(first, n, value, skip)
-            put(DENS, 1, d0)
-            put(DENS + 1, 1, d1)
-            put(POP, 1, pops[0, way, x])
-            put(POP + 1, 1, pops[1, way, x])
-            put(SOLID, 1, sd)
-            put(SOLID + 1, 2, sd)
-        return 0
-
-    lax.fori_loop(0, nx, row, 0, unroll=4)
+            for species in range(2):
+                put(DENS + species, 1, d[species])
+                put(POP + species, 1, pops[species, way, x])
+            put(SOLID, 1, solid[x])
+            put(SOLID + 1, 2, solid[x])
+
+
+def at_rest(species, way, current, dens):
+    return current - (1.0 / RELAX_TIME[species]) * (current - WEIGHTS[way] * dens)
+
+
+def response(species, dens):
+    return (0.5 * 4.0 * WEIGHTS[1] * DRIFT_COEF[species] / RELAX_TIME[species]) * dens
+
+
+def prepare_kernel(pops, solids, base, gain, blocks, rest, resp):
+    nx, _, nz = solids.shape
+    lane = lax.broadcasted_iota(jnp.int32, (T, nz), 1)
+    line = lax.broadcasted_iota(jnp.int32, (T, nz), 0)
+    for x in range(nx):
+        for species in range(2):
+            dens = density(pops, species, x)
+            resp[species, x] = response(species, dens)
+            for i in range(7):
+                rest[species, i, x] = at_rest(species, i, pops[species, i, x], dens)
+    shifts = (None, None, None, (1, 0, line == 0), (T - 1, 0, line == T - 1),
+              (1, 1, lane == 0), (nz - 1, 1, lane == nz - 1))
+    for x in range(nx):
+        solid = solids[x]
+        free = 1.0 - solid
+        for i in range(1, 7):
+            sign = 1.0 if i % 2 == 1 else -1.0
+            opposite = OPPOSITE[i]
+            if i < 3:
+                source = x - 1 if i == 1 else x + 1
+                inside = 0 <= source < nx
+                block = solids[source] if inside else jnp.ones_like(solid)
+
+                def moved(value, index):
+                    return value[(*index, source)]
+            else:
+                by, axis, border = shifts[i]
+                inside = True
+                block = jnp.where(border, 1.0, pltpu.roll(solid, by, axis))
+
+                def moved(value, index):
+                    return pltpu.roll(value[(*index, x)], by, axis)
+            blocks[i - 1, x] = block
+            for species in range(2):
+                own, back = rest[species, opposite, x], resp[species, x]
+                if inside:
+                    own = jnp.where(block > 0.5, own, moved(rest, (species, i)))
+                    back = jnp.where(block > 0.5, -back, moved(resp, (species,)))
+                else:
+                    back = -back
+                base[species, i, x] = free * own
+                gain[species, i - 1, x] = (sign * free) * back
+        for species in range(2):
+            base[species, 0, x] = free * rest[species, 0, x]
 
 
 def x_row(buf, side, name, distance):
@@ -135,7 +178,7 @@
     return buf[first + (n - distance if side == 0 else distance - 1)]
 
 
-def corner_kernel(xlo, xhi, mate, other):
+def corner_kernel(xlo, xhi, blocks, mate, other):
     on_parity(lambda lo, hi: pack_corners(xlo, xhi, (mate, other)[lo], (mate, other)[hi]))
 
 
@@ -201,8 +244,8 @@
     lax.fori_loop(0, nx, own, 0, unroll=4)
 
 
-def inner_kernel(sigma, charge, flags, prev, mate, other,
-                 pv, sg, un, wx, wy, wz, v0, v1, v2, ch, sums, rest_lo, rest_hi):
+def start_kernel(sigma, charge, flags, prev, mate, other,
+                 pv, sg, un, wx, wy, wz, v0, ch, rest_lo, rest_hi):
     nx, _, nz = sigma.shape
     top = nx + H
     first, last = ends(nz)
@@ -218,24 +261,35 @@
 
     lax.fori_loop(H, top, faces, sg[H], unroll=4)
 
-    def sweep(src, lo, hi, store, unroll):
-        def body(x, below):
-            value, below = laplace(src[x], src[x + 1], below, wx[x], wy[x], wz[x], sg[x], first, last)
-            store(x, value)
-            return below
-        lax.fori_loop(lo, hi, body, wx[lo - 1] * (src[lo - 1] - src[lo]), unroll=unroll)
-
     def store_v0(x, value):
         v0[x] = un[x] * (ch[x] - value)
+
+    inner_sweep(pv, H + 1, top - 1, store_v0, 7, wx, wy, wz, sg)
+
+
+def inner_sweep(src, lo, hi, store, unroll, wx, wy, wz, sg):
+    first, last = ends(src.shape[2])
+
+    def body(x, below):
+        value, below = laplace(src[x], src[x + 1], below, wx[x], wy[x], wz[x], sg[x], first, last)
+        store(x, value)
+        return below
+
+    lax.fori_loop(lo, hi, body, wx[lo - 1] * (src[lo - 1] - src[lo]), unroll=unroll)
+
+
+def inner_kernel(sg, un, wx, wy, wz, v0, v1, v2, sums):
+    nx, nz = sg.shape[0] - 2 * H, sg.shape[2]
+    top = nx + H
+    first, last = ends(nz)
 
     def apply_to(src, dst):
         def store(x, value):
             dst[x] = mapped(un[x], value, src[x])
         return store
 
-    sweep(pv, H + 1, top - 1, store_v0, 7)
-    sweep(v0, H + 2, top - 2, apply_to(v0, v1), 6)
-    sweep(v1, H + 3, top - 3, apply_to(v1, v2), 5)
+    inner_sweep(v0, H + 2, top - 2, apply_to(v0, v1), 6, wx, wy, wz, sg)
+    inner_sweep(v1, H + 3, top - 3, apply_to(v1, v2), 5, wx, wy, wz, sg)
 
     def last_sweep(x, carry):
         below, acc = carry
@@ -251,7 +305,7 @@
         sums[k] = value
 
 
-def outer_kernel(pv_in, sg_in, un_in, wx_in, wy_in, wz_in, v0_in, v1_in, v2_in, ch_in, sums,
+def outer_kernel(pv_in, sg_in, un_in, wx_in, wy_in, wz_in, v0_in, ch_in, v1_in, v2_in, sums,
                  xlo, xhi, mate, other,
                  pv_out, v0_out, v1_out, v2_out, moments, sg_out, un_out, ch_out, wx_out, wy_out, wz_out):
     nx, nz = pv_in.shape[0] - 2 * H, pv_in.shape[2]
@@ -372,123 +426,86 @@
     return (a0 + a1 * p1[0] + a2 * p2[0], a1 * p1[1] + a2 * p2[1], a2 * p2[2])
 
 
-def step_kernel(moments, pops, solids, pv, v0, v1, v2, pv_x, v0_x, v1_x, v2_x, xlo, xhi, ylo, yhi,
-                potential_hbm, nxt_hbm, pot, coll, nxt, potential, sem):
+def step_kernel(moments, base, gain, blocks, solids, pv, v0, v1, v2, pv_x, v0_x, v1_x, v2_x, xlo, xhi, rest_lo, rest_hi,
+                potential_hbm, nxt_hbm, pot, nxt, potential, sem):
     nx, _, nz = solids.shape
     top = nx + H
+    copies = [pltpu.make_async_copy(base.at[:, 0], nxt_hbm.at[:, 0], sem.at[1])]
+    copies[0].start()
     row = jnp.sum(moments[...], axis=0, keepdims=True)
     col = lax.broadcasted_iota(jnp.int32, (1, 128), 1)
     mu = [jnp.sum(jnp.where(col == k, row, 0.0), axis=1, keepdims=True) for k in range(6)]
     coef = [c * SCALE for c in cg_coefficients(mu)]
 
-    def corrected(p, a, b, c):
-        return p + (coef[0] * a + coef[1] * b + coef[2] * c)
-
-    def correct(x, _):
-        pot[x] = corrected(pv[x], v0[x], v1[x], v2[x])
-        return 0
-
-    lax.fori_loop(H + 3, top - 3, correct, 0, unroll=5)
-    for x in (*range(H - 2, H + 3), *range(top - 3, top + 2)):
+    def correct(x):
         depth = min(x - H, top - 1 - x)
         out = x if x < 8 else x - (nx + 2 * H - 16)
-        pot[x] = corrected(
-            pv[x] if depth >= 0 else pv_x[out],
-            v0[x] if depth >= 1 else v0_x[out],
-            v1[x] if depth >= 2 else v1_x[out],
-            v2_x[out],
-        )
+        fields = ((v0, v0_x), (v1, v1_x), (v2, v2_x))
+        terms = [
+            c * (a[x] if depth > k else b[out]) for k, (c, (a, b)) in enumerate(zip(coef, fields))
+        ]
+        pot[x] = (pv[x] if depth >= 0 else pv_x[out]) + (terms[0] + terms[1] + terms[2])
 
     lane = lax.broadcasted_iota(jnp.int32, (T, nz), 1)
     line = lax.broadcasted_iota(jnp.int32, (T, nz), 0)
 
-    def moved(species, way, current, density, grad):
+    def entering(species, way, current, dens, difference):
         sign = 1.0 if way % 2 == 1 else -1.0
-        velocity = sign * (DRIFT_COEF[species] * grad)
-        balance = WEIGHTS[way] * density * (1.0 + 4.0 * velocity)
-        return current - (1.0 / RELAX_TIME[species]) * (current - balance)
-
-    for species in range(2):
-        grad = 0.5 * (pot[H, T:2 * T] - pot[H - 2, T:2 * T])
-        coll[species, 1, 0] = moved(species, 1, xlo[POP + species], xlo[DENS + species], grad)
-        grad = 0.5 * (pot[top + 1, T:2 * T] - pot[top - 1, T:2 * T])
-        coll[species, 2, nx + 1] = moved(species, 2, xhi[POP + species], xhi[DENS + species], grad)
-
-    def collide(x):
+        return at_rest(species, way, current, dens) + sign * response(species, dens) * difference
+
+    def step(x):
         at = x + H
-        wide = pot[at]
-        mid = wide[T:2 * T]
+        mid = pot[at, T:2 * T]
         potential[x] = mid
-        gx = 0.5 * (pot[at + 1, T:2 * T] - pot[at - 1, T:2 * T])
-        gy = 0.5 * (pltpu.roll(wide, 3 * T - 1, 0)[T:2 * T] - pltpu.roll(wide, 1, 0)[T:2 * T])
-        gz = 0.5 * (jnp.where(lane == nz - 1, 0.0, pltpu.roll(mid, nz - 1, 1))
-                    - jnp.where(lane == 0, 0.0, pltpu.roll(mid, 1, 1)))
-        grads = (None, gx, gx, gy, gy, gz, gz)
+        free = 1.0 - solids[x]
+        dx = [pot[at + 1 + k, T:2 * T] - pot[at - 1 + k, T:2 * T] for k in (0, -1, 1)]
+        near = {k: pot[at, T + k:2 * T + k] for k in (-2, -1, 1, 2)}
+        dy = (near[1] - near[-1], mid - near[-2], near[2] - mid)
+        dz = (jnp.where(lane == nz - 1, 0.0, pltpu.roll(mid, nz - 1, 1))
+              - jnp.where(lane == 0, 0.0, pltpu.roll(mid, 1, 1)))
+        dz = (dz, pltpu.roll(dz, 1, 1), pltpu.roll(dz, nz - 1, 1))
+        difference = [None]
+        for d in (dx, dy, dz):
+            for k in (1, 2):
+                block = blocks[len(difference) - 1, x]
+                difference.append(jnp.where(block > 0.5, d[0], d[k]))
         for species in range(2):
-            current = [pops[species, i, x] for i in range(7)]
-            density = current[0]
             for i in range(1, 7):
-                density = density + current[i]
-            rate = 1.0 / RELAX_TIME[species]
-            coll[species, 0, x + 1] = current[0] - rate * (current[0] - WEIGHTS[0] * density)
-            for i in range(1, 7):
-                coll[species, i, x + 1] = moved(species, i, current[i], density, grads[i])
-
-    def stream(x):
-        at = x + H
-        solid = solids[x]
-        below = jnp.where(x == 0, xlo[SOLID], solids[jnp.maximum(x - 1, 0)])
-        above = jnp.where(x == nx - 1, xhi[SOLID], solids[jnp.minimum(x + 1, nx - 1)])
-        blocked = (
-            None,
-            below > 0.5,
-            above > 0.5,
-            jnp.where(line == 0, ylo[x, SOLID - 2 * T:SOLID - 2 * T + 1], pltpu.roll(solid, 1, 0)) > 0.5,
-            jnp.where(line == T - 1, yhi[x, SOLID - 2 * T:SOLID - 2 * T + 1], pltpu.roll(solid, T - 1, 0)) > 0.5,
-            jnp.where(lane == 0, 1.0, pltpu.roll(solid, 1, 1)) > 0.5,
-            jnp.where(lane == nz - 1, 1.0, pltpu.roll(solid, nz - 1, 1)) > 0.5,
-        )
-        free = 1.0 - solid
-        grad_lo = 0.5 * (pot[at, T:T + 1] - pot[at, T - 2:T - 1])
-        grad_hi = 0.5 * (pot[at, 2 * T + 1:2 * T + 2] - pot[at, 2 * T - 1:2 * T])
+                value = base[species, i, x] + gain[species, i - 1, x] * difference[i]
+                if i in (3, 4):
+                    rest, border, d = ((rest_lo, 0, dy[1]), (rest_hi, T - 1, dy[2]))[i - 3]
+
+                    def face(first):
+                        first -= 2 * T
+                        return rest[x, first:first + 1]
+                    here = slice(border, border + 1)
+                    new = entering(species, i, face(POP + species), face(DENS + species), d[here])
+                    new = jnp.where(face(SOLID) > 0.5, value[here], free[here] * new)
+                    value = jnp.where(line == border, new, value)
+                nxt[species, i - 1, x] = value
+
+    def x_face(x, way, buf, d):
+        free = 1.0 - solids[x]
         for species in range(2):
-            c = [None] + [coll[species, i, x + 1] for i in range(1, 7)]
-            from_lo = moved(species, 3, ylo[x, POP - 2 * T + species:POP - 2 * T + species + 1],
-                            ylo[x, DENS - 2 * T + species:DENS - 2 * T + species + 1], grad_lo)
-            from_hi = moved(species, 4, yhi[x, POP - 2 * T + species:POP - 2 * T + species + 1],
-                            yhi[x, DENS - 2 * T + species:DENS - 2 * T + species + 1], grad_hi)
-            source = (
-                None,
-                coll[species, 1, x],
-                coll[species, 2, x + 2],
-                jnp.where(line == 0, from_lo, pltpu.roll(c[3], 1, 0)),
-                jnp.where(line == T - 1, from_hi, pltpu.roll(c[4], T - 1, 0)),
-                pltpu.roll(c[5], 1, 1),
-                pltpu.roll(c[6], nz - 1, 1),
-            )
-            nxt[species, 0, x] = coll[species, 0, x + 1] * free
-            for i in range(1, 7):
-                nxt[species, i, x] = jnp.where(blocked[i], c[OPPOSITE[i]], source[i]) * free
-
-    def both(x, _):
-        collide(x + 1)
-        stream(x)
-        return 0
-
-    collide(0)
-    quarter = nx // 4
-    copies = []
-    for q in range(4):
-        end = (q + 1) * quarter
-        lax.fori_loop(q * quarter, min(end, nx - 1), both, 0)
-        if end == nx:
-            stream(nx - 1)
-        rows = pl.ds(q * quarter, quarter)
-        copies.append(pltpu.make_async_copy(nxt.at[:, :, rows], nxt_hbm.at[:, :, rows], sem.at[q]))
+            new = entering(species, way, buf[POP + species], buf[DENS + species], d)
+            nxt[species, way - 1, x] = jnp.where(buf[SOLID] > 0.5, nxt[species, way - 1, x], free * new)
+
+    for x in range(H - 2, H + 2):
+        correct(x)
+    for first in range(0, nx, 2):
+        for x in range(first, first + 2):
+            correct(x + H + 2)
+            step(x)
+        if first == 0:
+            x_face(0, 1, xlo, pot[H, T:2 * T] - pot[H - 2, T:2 * T])
+        if first == nx - 2:
+            x_face(nx - 1, 2, xhi, pot[top + 1, T:2 * T] - pot[top - 1, T:2 * T])
+        rows = pl.ds(first, 2)
+        copies.append(pltpu.make_async_copy(
+            nxt.at[:, :, rows], nxt_hbm.at[:, 1:, rows], sem.at[2 + first // 2]))
         copies[-1].start()
-        if end == nx:
-            copies.append(pltpu.make_async_copy(potential, potential_hbm, sem.at[4]))
-            copies[-1].start()
+    copies.append(pltpu.make_async_copy(potential, potential_hbm, sem.at[0]))
+    copies[-1].start()
     for copy in copies:
         copy.wait()
 
@@ -514,55 +531,70 @@
     x_face = jax.ShapeDtypeStruct((22, ny, nz), F32)
     y_face = jax.ShapeDtypeStruct((nx, FACE_ROWS, nz), F32)
     whole = jax.ShapeDtypeStruct(populations.shape, F32)
-    pops, sigma, solid, flags, prev, charge, xlo_s, xhi_s = pl.pallas_call(
+    arguments = (
+        pltpu.with_memory_space_constraint(a, pltpu.HBM)
+        for a in (populations, conductivity, deposit_mask, electrode_flags, previous_potential)
+    )
+    pops, sigma, solid, flags, prev, charge, xlo_s, xhi_s, y_mate, y_other = pl.pallas_call(
         load_kernel,
-        out_shape=(whole, brick, brick, brick, brick, brick, x_face, x_face),
+        out_shape=(whole, brick, brick, brick, brick, brick, x_face, x_face, y_face, y_face),
         in_specs=[HBM] * 5,
-        out_specs=(VMEM,) * 8,
+        out_specs=(VMEM,) * 10,
         scratch_shapes=[
-            pltpu.VMEM(conductivity.shape, F32),
-            pltpu.VMEM(conductivity.shape, jnp.int32),
-            pltpu.VMEM(conductivity.shape, jnp.int32),
+            pltpu.VMEM((nx, ny, nz), F32),
+            pltpu.VMEM((nx, ny, nz), jnp.int32),
+            pltpu.VMEM((nx, ny, nz), jnp.int32),
             pltpu.SemaphoreType.DMA((8,)),
         ],
         compiler_params=params(16),
         name="load",
-    )(*(pltpu.with_memory_space_constraint(a, pltpu.HBM) for a in (
-        populations, conductivity, deposit_mask, electrode_flags, previous_potential)))
+    )(*arguments)
     xlo = shift(xhi_s, "gx", 1)
     xhi = shift(xlo_s, "gx", -1)
-    y_mate, y_other = pl.pallas_call(
-        pack_kernel,
-        out_shape=(y_face, y_face),
-        in_specs=[VMEM] * 6,
-        out_specs=(VMEM,) * 2,
-        compiler_params=params(16),
-        name="pack",
-    )(pops, sigma, solid, flags, prev, charge)
     y_mate = to_mate(y_mate)
     y_other = to_other(y_other)
+    six = jax.ShapeDtypeStruct((2, 6, nx, ny, nz), F32)
+    base, gain, blocks = pl.pallas_call(
+        prepare_kernel,
+        out_shape=(whole, six, jax.ShapeDtypeStruct((6, nx, ny, nz), F32)),
+        in_specs=[VMEM] * 2,
+        out_specs=(VMEM,) * 3,
+        scratch_shapes=[pltpu.VMEM(whole.shape, F32), pltpu.VMEM((2, nx, ny, nz), F32)],
+        compiler_params=params(24),
+        name="prepare",
+    )(pops, solid)
+    shape = (nx + 2 * H, 3 * T, nz)
+    padded = jax.ShapeDtypeStruct(shape, F32)
+    *fields, rest_lo, rest_hi = pl.pallas_call(
+        start_kernel,
+        out_shape=(padded,) * 8 + (brick, brick),
+        in_specs=[VMEM] * 6,
+        out_specs=(VMEM,) * 10,
+        compiler_params=params(24),
+        cost_estimate=pl.CostEstimate(flops=60_000_000, bytes_accessed=20_000_000, transcendentals=0),
+        name="start",
+    )(sigma, charge, flags, prev, y_mate, y_other)
+    pv, sg, un, wx, wy, wz, v0, _ = fields
     corner = jax.ShapeDtypeStruct((8, ny, nz), F32)
     c_mate, c_other = pl.pallas_call(
         corner_kernel,
         out_shape=(corner, corner),
-        in_specs=[VMEM] * 2,
+        in_specs=[VMEM] * 2 + [pl.BlockSpec(memory_space=pl.ANY)],
         out_specs=(VMEM,) * 2,
         compiler_params=params(8),
         name="corners",
-    )(xlo, xhi)
+    )(xlo, xhi, blocks)
     c_mate = to_mate(c_mate)
     c_other = to_other(c_other)
-    shape = (nx + 2 * H, 3 * T, nz)
-    padded = jax.ShapeDtypeStruct(shape, F32)
-    *inner, rest_lo, rest_hi = pl.pallas_call(
+    v1, v2, sums = pl.pallas_call(
         inner_kernel,
-        out_shape=(padded,) * 10 + (jax.ShapeDtypeStruct((6, ny, nz), F32), brick, brick),
+        out_shape=(padded, padded, jax.ShapeDtypeStruct((6, ny, nz), F32)),
         in_specs=[VMEM] * 6,
-        out_specs=(VMEM,) * 13,
+        out_specs=(VMEM,) * 3,
         compiler_params=params(24),
         cost_estimate=pl.CostEstimate(flops=60_000_000, bytes_accessed=20_000_000, transcendentals=0),
         name="inner",
-    )(sigma, charge, flags, prev, y_mate, y_other)
+    )(sg, un, wx, wy, wz, v0)
     outer_shape = (16, 3 * T, nz)
     edges = jax.ShapeDtypeStruct(outer_shape, F32)
     count = lax.axis_size("gx") * lax.axis_size("gy")
@@ -574,24 +606,22 @@
         scratch_shapes=[pltpu.VMEM(outer_shape, F32)] * 6,
         compiler_params=params(28),
         name="outer",
-    )(*inner, xlo, xhi, c_mate, c_other)
+    )(*fields, v1, v2, sums, xlo, xhi, c_mate, c_other)
     moments = lax.all_to_all(moments, ("gx", "gy"), 0, 0, tiled=True)
-    pv, v0, v1, v2 = (inner[i] for i in (0, 6, 7, 8))
     return pl.pallas_call(
         step_kernel,
         out_shape=(brick, whole),
-        in_specs=[VMEM] * 15,
+        in_specs=[VMEM] * 17,
         out_specs=(HBM,) * 2,
         scratch_shapes=[
             pltpu.VMEM(shape, F32),
-            pltpu.VMEM((2, 7, nx + 2, ny, nz), F32),
-            pltpu.VMEM(populations.shape, F32),
-            pltpu.VMEM(conductivity.shape, F32),
-            pltpu.SemaphoreType.DMA((5,)),
+            pltpu.VMEM(six.shape, F32),
+            pltpu.VMEM((nx, ny, nz), F32),
+            pltpu.SemaphoreType.DMA((2 + nx // 2,)),
         ],
         compiler_params=params(28),
         name="step",
-    )(moments, pops, solid, pv, v0, v1, v2, pv_x, v0_x, v1_x, v2_x, xlo, xhi, rest_lo, rest_hi)
+    )(moments, base, gain, blocks, solid, pv, v0, v1, v2, pv_x, v0_x, v1_x, v2_x, xlo, xhi, rest_lo, rest_hi)
 
 
 def solution(mesh):

time: 58.4 us -> 57.6 us (0.986)
  waiting for transfers between devices: 5.86 us -> 4.22 us
  Pallas kernels: 12.8 us -> 13.6 us
    ppermute x2, waiting for transfers between devices: 5.11 us -> 3.48 us  [shift(): lax.ppermute(block, axis, [(i, (i + distance) % n) for i in range(n)])]
    pallas_call x2 -> x3, Pallas kernels: 3.96 us -> 5.13 us  [the longest x1 1.82 us: local(): pl.pallas_call(start_kernel, out_shape=(padded,) * 8 + (brick, brick), in...]
  transfers between devices with their start and end apart: 6 -> 6, of which waited for: 2 -> 2; matrix products, arithmetic and copies ran while one was open for 0% -> 0% of each run, Pallas kernels for 6% -> 9%
where the time goes in v3:
time: 57.6 us; the launch traced here: 57.5 us
  blocking collectives  25.7 us (45%)
  Pallas kernels  13.6 us (24%)
  starting transfers between devices  13.3 us (23%)
  waiting for transfers between devices  4.22 us (7%)
  between operations  0.69 us (1%)
    all_to_all x1, blocking collectives, local(): moments = lax.all_to_all(moments, ('gx', 'gy'), 0, 0, tiled=True)  25.7 us
    ppermute x2, starting transfers between devices, to_mate(): return lax.ppermute(block, 'gy', [(i, i ^ 1) for i in range(n)])  8.12 us
    ppermute x2, starting transfers between devices, shift(): lax.ppermute(block, axis, [(i, (i + distance) % n) for i in range(n)])  5.04 us
    ppermute x2, waiting for transfers between devices, shift(): lax.ppermute(block, axis, [(i, (i + distance) % n) for i in range(n)])  3.48 us
    pallas_call x1, Pallas kernels, local(): pl.pallas_call(outer_kernel, out_shape=(edges,) * 4 + (jax.ShapeDtypeStru...  2.96 us
    pallas_call x1, Pallas kernels, local(): pl.pallas_call(step_kernel, out_shape=(brick, whole), in_specs=[VMEM] * 1...  2.96 us
    pallas_call x1, Pallas kernels, local(): pl.pallas_call(load_kernel, out_shape=(whole, brick, brick, brick, brick,...  2.53 us
    pallas_call x1, Pallas kernels, local(): pl.pallas_call(start_kernel, out_shape=(padded,) * 8 + (brick, brick), in...  1.82 us
  transfers between devices with their start and end apart: 6, of which 2 were waited for; matrix products, arithmetic and copies ran while one was open for 0% of the time, Pallas kernels for 9%

profile of v3, /device:TPU:1, one launch (start us, length us, event | category | flops | bytes accessed | tf_op | source)
XLA Modules:
  0.0 57.5 jit_solution(3165370522614000889)
XLA Ops:
  0.6 2.5 %load.1 = (f32[2,7,16,8,512]{4,3,2,1,0:T(8,128)S(1)}, f32[16,8,512]{2,1,0:T(8,128)S(1)}, f32[16,8,512]{2,1,0:T(8,128)S(1)}, f32[16,8,512]{2,1,0:T(8,128)S(1)}, f...) custom-call(f32[2,7,16,8,512]{4,3,2,1,0:T(8,128)} %pops_hbm.1, ...), custom_call_target="tpu_custom_call" | custom-call | tf_op jit(solution)/shard_map/load/pallas_call | solution.py:538
  3.2 3.3 %collective-permute-start = (f32[16,24,512]{2,1,0:T(8,128)S(1)}, f32[16,24,512]{2,1,0:T(8,128)S(1)}, u32[]{:S(2)}, u32[]{:S(2)}) collective-permute-start(f32[16,24,512]{2,1,0:T(8,128)S(1)} %get-tuple-element.39), channel_id=1, source_target_pairs={{0,1},{1,0},{2,3},{3,2},{4,5},{5,4},{6,7},{7,6},{8,9},{9,8},{10,11... | collective-permute-start | bytes 2359304 | tf_op jit(solution)/shard_map/ppermute | solution.py:515
  6.5 0.0 collective-permute-start.1
  6.5 1.1 %collective-permute-start.2 = (f32[22,8,512]{2,1,0:T(8,128)S(1)}, f32[22,8,512]{2,1,0:T(8,128)S(1)}, u32[]{:S(2)}, u32[]{:S(2)}) collective-permute-start(f32[22,8,512]{2,1,0:T(8,128)S(1)} %get-tuple-element.52), channel_id=1, source_target_pairs={{0,32},{32,64},{64,96},{96,128},{128,160},{160,192},{192,224},{224... | collective-permute-start | bytes 1081352 | tf_op jit(solution)/shard_map/ppermute | solution.py:525
  7.6 3.9 %collective-permute-start.3 = (f32[22,8,512]{2,1,0:T(8,128)S(1)}, f32[22,8,512]{2,1,0:T(8,128)S(1)}, u32[]{:S(2)}, u32[]{:S(2)}) collective-permute-start(f32[22,8,512]{2,1,0:T(8,128)S(1)} %get-tuple-element.53), channel_id=1, source_target_pairs={{0,224},{32,0},{64,32},{96,64},{128,96},{160,128},{192,160},{224,1... | collective-permute-start | bytes 1081352 | tf_op jit(solution)/shard_map/ppermute | solution.py:525
  11.5 1.6 %prepare.1 = (f32[2,7,16,8,512]{4,3,2,1,0:T(8,128)S(1)}, f32[2,6,16,8,512]{4,3,2,1,0:T(8,128)S(1)}, f32[6,16,8,512]{3,2,1,0:T(8,128)S(1)}) custom-call(f32[2,7,16,8,512]{4,3,2,1,0:T(8,128)S(1)} %get-tuple-element.54.pops, f32[16,8,512]{2,1,0:T(8,128)S(1)} %get-tuple-element.55.solids), custom_call_target="tpu_custom_call" | custom-call | tf_op jit(solution)/shard_map/prepare/pallas_call | solution.py:557
  13.2 3.5 %collective-permute-done.2.xlo = f32[22,8,512]{2,1,0:T(8,128)S(1)} collective-permute-done((f32[22,8,512]{2,1,0:T(8,128)S(1)}, f32[22,8,512]{2,1,0:T(8,128)S(1)}, u32[]{:S(2)}, u32[]{:S(2)}) %collective-permute-start.2) | collective-permute-done | bytes 360480 | tf_op jit(solution)/shard_map/ppermute | solution.py:525
  16.6 0.0 collective-permute-done.3.xhi
  16.6 0.1 corners.1
  16.7 4.8 %collective-permute-start.4 = (f32[8,8,512]{2,1,0:T(8,128)S(1)}, f32[8,8,512]{2,1,0:T(8,128)S(1)}, u32[]{:S(2)}, u32[]{:S(2)}) collective-permute-start(f32[8,8,512]{2,1,0:T(8,128)S(1)} %get-tuple-element.57), channel_id=1, source_target_pairs={{0,1},{1,0},{2,3},{3,2},{4,5},{5,4},{6,7},{7,6},{8,9},{9,8},{10,11... | collective-permute-start | bytes 393224 | tf_op jit(solution)/shard_map/ppermute | solution.py:515
  21.5 0.1 collective-permute-start.5
  21.6 0.0 collective-permute-done.mate
  21.6 0.0 collective-permute-done.1.other
  21.6 1.8 %start.1 = (f32[26,24,512]{2,1,0:T(8,128)S(1)}, f32[26,24,512]{2,1,0:T(8,128)S(1)}, f32[26,24,512]{2,1,0:T(8,128)S(1)}, f32[26,24,512]{2,1,0:T(8,128)S(1)}, f32[...) custom-call(f32[16,8,512]{2,1,0:T(8,128)S(1)} %get-tuple-element.35., ...), custom_call_target="tpu_custom_call" | custom-call | flops 60000000 | bytes 20000000 | tf_op jit(solution)/shard_map/start/pallas_call | solution.py:568
  23.5 1.7 %inner.1 = (f32[26,24,512]{2,1,0:T(8,128)S(1)}, f32[26,24,512]{2,1,0:T(8,128)S(1)}, f32[6,8,512]{2,1,0:T(8,128)S(1)}) custom-call(f32[26,24,512]{2,1,0:T(8,128)S(1)} %get-tuple-element.42.sg.sg_in, f32[26,24,512]{2,1,0:T(8,128)S(1)} %get-tuple-element.43.un.un_in, f32[26,24,512]{2,1,0:T(8,128)S(1)} %get-tuple-element.44.wx.wx_in, ...), custom_call_target="tpu_custom_call" | custom-call | flops 60000000 | bytes 20000000 | tf_op jit(solution)/shard_map/inner/pallas_call | solution.py:589
  25.2 0.0 collective-permute-done.4.mate
  25.2 0.7 %collective-permute-done.5.other = f32[8,8,512]{2,1,0:T(8,128)S(1)} collective-permute-done((f32[8,8,512]{2,1,0:T(8,128)S(1)}, f32[8,8,512]{2,1,0:T(8,128)S(1)}, u32[]{:S(2)}, u32[]{:S(2)}) %collective-permute-start.5) | collective-permute-done | bytes 131104 | tf_op jit(solution)/shard_map/ppermute | solution.py:520
  25.9 3.0 %outer.1 = (f32[16,24,512]{2,1,0:T(8,128)S(1)}, f32[16,24,512]{2,1,0:T(8,128)S(1)}, f32[16,24,512]{2,1,0:T(8,128)S(1)}, f32[16,24,512]{2,1,0:T(8,128)S(1)}, f32[256,128]{1,0:T(8,128)S(1)}) custom-call(f32[26,24,512]{2,1,0:T(8,128)S(1)} %get-tuple-element.41.pv_in.pv, f32[26,24,512]{2,1,0:T(8,128)S(1)} %get-tuple-element.42.sg.sg_in, ...), custom_call_target="tpu_custom_call" | custom-call | tf_op jit(solution)/shard_map/outer/pallas_call | solution.py:601
  28.9 25.7 %all_to_all.11 = f32[256,1,128]{2,1,0:T(1,128)S(1)} all-to-all(f32[256,1,128]{2,1,0:T(1,128)S(1)} %bitcast.5), channel_id=1, replica_groups=mesh['gx'=8,'gy'=32] {'gx','gy'}, dimensions={0} | all-to-all | bytes 262144 | tf_op jit(solution)/shard_map/all_to_all | solution.py:610
  54.6 3.0 %step.1 = (f32[16,8,512]{2,1,0:T(8,128)}, f32[2,7,16,8,512]{4,3,2,1,0:T(8,128)}) custom-call(f32[256,128]{1,0:T(8,128)S(1)} %bitcast.4, f32[2,7,16,8,512]{4,3,2,1,0:T(8,128)S(1)} %get-tuple-element.60.base, f32[2,6,16,8,512]{4,3,2,1,0:T(8,128)S(1)} %get-tuple-element.61.gain, f32[6,16,8,512]{3,2,1,0:T(8,128)S(1)} %get-tuple-element.56.blocks, ...), custom_call_target="tpu_custom_call" | custom-call | tf_op jit(solution)/shard_map/step/pallas_call | solution.py:611
Async XLA Ops:
  3.2 18.5 %collective-permute-start = (f32[16,24,512]{2,1,0:T(8,128)S(1)}, f32[16,24,512]{2,1,0:T(8,128)S(1)}, u32[]{:S(2)}, u32[]{:S(2)}) collective-permute-start(f32[16,24,512]{2,1,0:T(8,128)S(1)} %get-tuple-element.39), channel_id=1, source_target_pairs={{0,1},{1,0},{2,3},{3,2},{4,5},{5,4},{6,7},{7,6},{8,9},{9,8},{10,11... | collective-permute-start | bytes 2359304 | tf_op jit(solution)/shard_map/ppermute | solution.py:515
  6.5 15.1 %collective-permute-start.1 = (f32[16,24,512]{2,1,0:T(8,128)S(1)}, f32[16,24,512]{2,1,0:T(8,128)S(1)}, u32[]{:S(2)}, u32[]{:S(2)}) collective-permute-start(f32[16,24,512]{2,1,0:T(8,128)S(1)} %get-tuple-element.40), channel_id=1, source_target_pairs={{0,31},{1,2},{2,1},{3,4},{4,3},{5,6},{6,5},{7,8},{8,7},{9,10},{10,... | collective-permute-start | bytes 2359304 | tf_op jit(solution)/shard_map/ppermute | solution.py:520
  6.5 10.1 %collective-permute-start.2 = (f32[22,8,512]{2,1,0:T(8,128)S(1)}, f32[22,8,512]{2,1,0:T(8,128)S(1)}, u32[]{:S(2)}, u32[]{:S(2)}) collective-permute-start(f32[22,8,512]{2,1,0:T(8,128)S(1)} %get-tuple-element.52), channel_id=1, source_target_pairs={{0,32},{32,64},{64,96},{96,128},{128,160},{160,192},{192,224},{224... | collective-permute-start | bytes 1081352 | tf_op jit(solution)/shard_map/ppermute | solution.py:525
  7.6 9.0 %collective-permute-start.3 = (f32[22,8,512]{2,1,0:T(8,128)S(1)}, f32[22,8,512]{2,1,0:T(8,128)S(1)}, u32[]{:S(2)}, u32[]{:S(2)}) collective-permute-start(f32[22,8,512]{2,1,0:T(8,128)S(1)} %get-tuple-element.53), channel_id=1, source_target_pairs={{0,224},{32,0},{64,32},{96,64},{128,96},{160,128},{192,160},{224,1... | collective-permute-start | bytes 1081352 | tf_op jit(solution)/shard_map/ppermute | solution.py:525
  16.7 8.4 %collective-permute-start.4 = (f32[8,8,512]{2,1,0:T(8,128)S(1)}, f32[8,8,512]{2,1,0:T(8,128)S(1)}, u32[]{:S(2)}, u32[]{:S(2)}) collective-permute-start(f32[8,8,512]{2,1,0:T(8,128)S(1)} %get-tuple-element.57), channel_id=1, source_target_pairs={{0,1},{1,0},{2,3},{3,2},{4,5},{5,4},{6,7},{7,6},{8,9},{9,8},{10,11... | collective-permute-start | bytes 393224 | tf_op jit(solution)/shard_map/ppermute | solution.py:515
  21.5 4.4 %collective-permute-start.5 = (f32[8,8,512]{2,1,0:T(8,128)S(1)}, f32[8,8,512]{2,1,0:T(8,128)S(1)}, u32[]{:S(2)}, u32[]{:S(2)}) collective-permute-start(f32[8,8,512]{2,1,0:T(8,128)S(1)} %get-tuple-element.58), channel_id=1, source_target_pairs={{0,31},{1,2},{2,1},{3,4},{4,3},{5,6},{6,5},{7,8},{8,7},{9,10},{10,... | collective-permute-start | bytes 393224 | tf_op jit(solution)/shard_map/ppermute | solution.py:520

commit v4 on v3

--- a/solution.py
+++ b/solution.py
@@ -17,7 +17,9 @@
 
 PREV, SIGMA, FLAGS, CHARGE = (0, 5), (5, 5), (10, 4), (14, 3)
 DENS, POP, SOLID = 17, 19, 21
-FACE_ROWS = 24
+Y_CHARGE = (14, 4)
+Y_ROWS = 18
+EXTRAS = 5
 
 CORNER = (
     ("prev", 1, 4, 0, 0), ("prev", 2, 3, 0, 4), ("prev", 4, 1, 0, 7),
@@ -44,12 +46,12 @@
 
 def on_parity(run):
     odd = lax.rem(lax.axis_index("gy"), 2)
-    pl.when(odd == 0)(lambda: run(1, 0))
-    pl.when(odd == 1)(lambda: run(0, 1))
+    pl.when(odd == 0)(lambda: run(0, 1))
+    pl.when(odd == 1)(lambda: run(1, 0))
 
 
 def load_kernel(pops_hbm, cond_hbm, mask_hbm, flags_hbm, prev_hbm,
-                pops, sigma, solid, flags, prev, charge, xlo, xhi, mate, other, cond, mask, marks, sem):
+                pops, sigma, solid, flags, prev, charge, xlo, xhi, other, mate, extra_other, extra_mate, cond, mask, marks, sem):
     nx = sigma.shape[0]
     quarter = nx // 4
     small = [
@@ -83,7 +85,8 @@
         large[q].wait()
         rows = range(q * quarter, (q + 1) * quarter)
         on_parity(lambda lo, hi: pack_faces(
-            pops, sigma, solid, flags, prev, charge, (mate, other)[lo], (mate, other)[hi], rows))
+            pops, sigma, solid, flags, prev, charge, (other, mate)[lo], (other, mate)[hi],
+            (extra_other, extra_mate)[lo], (extra_other, extra_mate)[hi], rows))
         if q in (0, 3):
             out, up, way = (xlo, False, 2) if q == 0 else (xhi, True, 1)
             first, n = CHARGE
@@ -96,23 +99,20 @@
             out[SOLID] = solid[edge]
 
 
-def pack_faces(pops, sigma, solid, flags, prev, charge, ylo, yhi, rows):
+def pack_faces(pops, sigma, solid, flags, prev, charge, ylo, yhi, extra_lo, extra_hi, rows):
     for x in rows:
         d = (density(pops, 0, x), density(pops, 1, x))
         ch = 2.0 * d[0] - 2.0 * d[1]
         charge[x] = ch
         values = (prev[x], sigma[x], flags[x], ch)
-        for out, up, way in ((ylo, False, 4), (yhi, True, 3)):
-            def put(first, n, value, skip=0):
-                at = T - n - skip if up else skip
-                out[x, first:first + n] = value[at:at + n]
-            for value, (first, n), skip in zip(values, (PREV, SIGMA, FLAGS, CHARGE), (0, 0, 0, 1)):
-                put(first, n, value, skip)
-            for species in range(2):
-                put(DENS + species, 1, d[species])
-                put(POP + species, 1, pops[species, way, x])
-            put(SOLID, 1, solid[x])
-            put(SOLID + 1, 2, solid[x])
+        for out, extra, up, way in ((ylo, extra_lo, False, 4), (yhi, extra_hi, True, 3)):
+            for value, (first, n) in zip(values, (PREV, SIGMA, FLAGS, Y_CHARGE)):
+                at = T - n if up else 0
+                out[x * Y_ROWS + first:x * Y_ROWS + first + n] = value[at:at + n]
+            at = T - 1 if up else 0
+            last = (*d, pops[0, way, x], pops[1, way, x], solid[x])
+            for k, value in enumerate(last):
+                extra[k, x:x + 1] = value[at:at + 1]
 
 
 def at_rest(species, way, current, dens):
@@ -178,8 +178,10 @@
     return buf[first + (n - distance if side == 0 else distance - 1)]
 
 
-def corner_kernel(xlo, xhi, blocks, mate, other):
-    on_parity(lambda lo, hi: pack_corners(xlo, xhi, (mate, other)[lo], (mate, other)[hi]))
+def corner_kernel(xlo, xhi, extra_other, extra_mate, blocks, other, mate, other_out, mate_out):
+    other_out[...] = extra_other[...]
+    mate_out[...] = extra_mate[...]
+    on_parity(lambda lo, hi: pack_corners(xlo, xhi, (other, mate)[lo], (other, mate)[hi]))
 
 
 def pack_corners(xlo, xhi, clo, chi):
@@ -218,39 +220,27 @@
     return (a * a, a * b, b * b, b * c, c * c, c * d)
 
 
-def place_faces(sigma, charge, flags, prev, ylo, yhi, pv, sg, un, ch, rest_lo, rest_hi):
-    nx = sigma.shape[0]
-
-    def own(x, _):
+def place_faces(sigma, charge, flags, prev, ylo, yhi, pv, sg, un, ch):
+    for x in range(sigma.shape[0]):
         at = x + H
         pv[at, T:2 * T] = prev[x]
         sg[at, T:2 * T] = sigma[x]
         un[at, T:2 * T] = 1.0 - flags[x]
         ch[at, T:2 * T] = charge[x]
-        for buf, up, rest in ((ylo, False, rest_lo), (yhi, True, rest_hi)):
-            rest[x] = buf[x, 2 * T:3 * T]
-            def put(ref, first, n, skip=0, one=False):
-                to = 2 * T + skip if up else T - n - skip
-                value = buf[x, first:first + n]
-                ref[at, to:to + n] = 1.0 - value if one else value
-            put(pv, *PREV)
-            put(sg, *SIGMA)
-            put(un, *FLAGS, 0, True)
-            put(ch, *CHARGE, 1)
-            to = 2 * T if up else T - 1
-            ch[at, to:to + 1] = 2.0 * buf[x, DENS:DENS + 1] - 2.0 * buf[x, DENS + 1:DENS + 2]
-        return 0
-
-    lax.fori_loop(0, nx, own, 0, unroll=4)
-
-
-def start_kernel(sigma, charge, flags, prev, mate, other,
-                 pv, sg, un, wx, wy, wz, v0, ch, rest_lo, rest_hi):
+        for buf, up in ((ylo, False), (yhi, True)):
+            for ref, (first, n) in ((pv, PREV), (sg, SIGMA), (un, FLAGS), (ch, Y_CHARGE)):
+                to = 2 * T if up else T - n
+                value = buf[x * Y_ROWS + first:x * Y_ROWS + first + n]
+                ref[at, to:to + n] = 1.0 - value if ref is un else value
+
+
+def start_kernel(sigma, charge, flags, prev, other, mate,
+                 pv, sg, un, wx, wy, wz, v0, ch):
     nx, _, nz = sigma.shape
     top = nx + H
     first, last = ends(nz)
     on_parity(lambda lo, hi: place_faces(
-        sigma, charge, flags, prev, (mate, other)[lo], (mate, other)[hi], pv, sg, un, ch, rest_lo, rest_hi))
+        sigma, charge, flags, prev, (other, mate)[lo], (other, mate)[hi], pv, sg, un, ch))
 
     def faces(x, a):
         b = sg[jnp.minimum(x + 1, top - 1)]
@@ -306,7 +296,7 @@
 
 
 def outer_kernel(pv_in, sg_in, un_in, wx_in, wy_in, wz_in, v0_in, ch_in, v1_in, v2_in, sums,
-                 xlo, xhi, mate, other,
+                 xlo, xhi, other, mate,
                  pv_out, v0_out, v1_out, v2_out, moments, sg_out, un_out, ch_out, wx_out, wy_out, wz_out):
     nx, nz = pv_in.shape[0] - 2 * H, pv_in.shape[2]
     top = nx + H
@@ -352,7 +342,7 @@
         for side in range(2):
             for name, distance, n, tile, row in CORNER:
                 ref = {"prev": pv_out, "sigma": sg_out, "flags": un_out, "charge": ch_out}[name]
-                for buf, to in (((mate, other)[lo], T - n), ((mate, other)[hi], 2 * T)):
+                for buf, to in (((other, mate)[lo], T - n), ((other, mate)[hi], 2 * T)):
                     value = buf[4 * side + tile, row:row + n]
                     ref[row_at(side, distance), to:to + n] = 1.0 - value if name == "flags" else value
 
@@ -426,12 +416,18 @@
     return (a0 + a1 * p1[0] + a2 * p2[0], a1 * p1[1] + a2 * p2[1], a2 * p2[2])
 
 
-def step_kernel(moments, base, gain, blocks, solids, pv, v0, v1, v2, pv_x, v0_x, v1_x, v2_x, xlo, xhi, rest_lo, rest_hi,
-                potential_hbm, nxt_hbm, pot, nxt, potential, sem):
+def step_kernel(moments, base, gain, blocks, solids, pv, v0, v1, v2, pv_x, v0_x, v1_x, v2_x, xlo, xhi, extra_other, extra_mate,
+                potential_hbm, nxt_hbm, pot, nxt, potential, rest_lo, rest_hi, sem):
     nx, _, nz = solids.shape
     top = nx + H
     copies = [pltpu.make_async_copy(base.at[:, 0], nxt_hbm.at[:, 0], sem.at[1])]
     copies[0].start()
+
+    def place_extras(lo, hi):
+        rest_lo[...] = (extra_other, extra_mate)[lo][...]
+        rest_hi[...] = (extra_other, extra_mate)[hi][...]
+
+    on_parity(place_extras)
     row = jnp.sum(moments[...], axis=0, keepdims=True)
     col = lax.broadcasted_iota(jnp.int32, (1, 128), 1)
     mu = [jnp.sum(jnp.where(col == k, row, 0.0), axis=1, keepdims=True) for k in range(6)]
@@ -476,8 +472,7 @@
                     rest, border, d = ((rest_lo, 0, dy[1]), (rest_hi, T - 1, dy[2]))[i - 3]
 
                     def face(first):
-                        first -= 2 * T
-                        return rest[x, first:first + 1]
+                        return rest[first - DENS, x:x + 1]
                     here = slice(border, border + 1)
                     new = entering(species, i, face(POP + species), face(DENS + species), d[here])
                     new = jnp.where(face(SOLID) > 0.5, value[here], free[here] * new)
@@ -529,17 +524,18 @@
     nx, ny, nz = conductivity.shape
     brick = jax.ShapeDtypeStruct((nx, ny, nz), F32)
     x_face = jax.ShapeDtypeStruct((22, ny, nz), F32)
-    y_face = jax.ShapeDtypeStruct((nx, FACE_ROWS, nz), F32)
+    y_face = jax.ShapeDtypeStruct((nx * Y_ROWS, nz), F32)
+    extra = jax.ShapeDtypeStruct((EXTRAS, nx, nz), F32)
     whole = jax.ShapeDtypeStruct(populations.shape, F32)
     arguments = (
         pltpu.with_memory_space_constraint(a, pltpu.HBM)
         for a in (populations, conductivity, deposit_mask, electrode_flags, previous_potential)
     )
-    pops, sigma, solid, flags, prev, charge, xlo_s, xhi_s, y_mate, y_other = pl.pallas_call(
+    pops, sigma, solid, flags, prev, charge, xlo_s, xhi_s, y_other, y_mate, e_other, e_mate = pl.pallas_call(
         load_kernel,
-        out_shape=(whole, brick, brick, brick, brick, brick, x_face, x_face, y_face, y_face),
+        out_shape=(whole, brick, brick, brick, brick, brick, x_face, x_face, y_face, y_face, extra, extra),
         in_specs=[HBM] * 5,
-        out_specs=(VMEM,) * 10,
+        out_specs=(VMEM,) * 12,
         scratch_shapes=[
             pltpu.VMEM((nx, ny, nz), F32),
             pltpu.VMEM((nx, ny, nz), jnp.int32),
@@ -551,8 +547,8 @@
     )(*arguments)
     xlo = shift(xhi_s, "gx", 1)
     xhi = shift(xlo_s, "gx", -1)
+    y_other = to_other(y_other)
     y_mate = to_mate(y_mate)
-    y_other = to_other(y_other)
     six = jax.ShapeDtypeStruct((2, 6, nx, ny, nz), F32)
     base, gain, blocks = pl.pallas_call(
         prepare_kernel,
@@ -565,27 +561,30 @@
     )(pops, solid)
     shape = (nx + 2 * H, 3 * T, nz)
     padded = jax.ShapeDtypeStruct(shape, F32)
-    *fields, rest_lo, rest_hi = pl.pallas_call(
+    fields = pl.pallas_call(
         start_kernel,
-        out_shape=(padded,) * 8 + (brick, brick),
+        out_shape=(padded,) * 8,
         in_specs=[VMEM] * 6,
-        out_specs=(VMEM,) * 10,
+        out_specs=(VMEM,) * 8,
         compiler_params=params(24),
         cost_estimate=pl.CostEstimate(flops=60_000_000, bytes_accessed=20_000_000, transcendentals=0),
         name="start",
-    )(sigma, charge, flags, prev, y_mate, y_other)
+    )(sigma, charge, flags, prev, y_other, y_mate)
     pv, sg, un, wx, wy, wz, v0, _ = fields
     corner = jax.ShapeDtypeStruct((8, ny, nz), F32)
-    c_mate, c_other = pl.pallas_call(
+    c_other, c_mate, e_other, e_mate = pl.pallas_call(
         corner_kernel,
-        out_shape=(corner, corner),
-        in_specs=[VMEM] * 2 + [pl.BlockSpec(memory_space=pl.ANY)],
-        out_specs=(VMEM,) * 2,
+        out_shape=(corner, corner, extra, extra),
+        in_specs=[VMEM] * 4 + [pl.BlockSpec(memory_space=pl.ANY)],
+        out_specs=(VMEM,) * 4,
+        cost_estimate=pl.CostEstimate(flops=20_000_000_000, bytes_accessed=300_000_000, transcendentals=0),
         compiler_params=params(8),
         name="corners",
-    )(xlo, xhi, blocks)
+    )(xlo, xhi, e_other, e_mate, blocks)
+    c_other = to_other(c_other)
     c_mate = to_mate(c_mate)
-    c_other = to_other(c_other)
+    e_other = to_other(e_other)
+    e_mate = to_mate(e_mate)
     v1, v2, sums = pl.pallas_call(
         inner_kernel,
         out_shape=(padded, padded, jax.ShapeDtypeStruct((6, ny, nz), F32)),
@@ -605,8 +604,10 @@
         out_specs=(VMEM,) * 5,
         scratch_shapes=[pltpu.VMEM(outer_shape, F32)] * 6,
         compiler_params=params(28),
+        cost_estimate=pl.CostEstimate(flops=20_000_000_000, bytes_accessed=300_000_000, transcendentals=0),
         name="outer",
-    )(*fields, v1, v2, sums, xlo, xhi, c_mate, c_other)
+    )(*fields, v1, v2, sums, xlo, xhi, c_other, c_mate)
+    moments, e_other, e_mate = lax.optimization_barrier((moments, e_other, e_mate))
     moments = lax.all_to_all(moments, ("gx", "gy"), 0, 0, tiled=True)
     return pl.pallas_call(
         step_kernel,
@@ -617,11 +618,13 @@
             pltpu.VMEM(shape, F32),
             pltpu.VMEM(six.shape, F32),
             pltpu.VMEM((nx, ny, nz), F32),
+            pltpu.VMEM(extra.shape, F32),
+            pltpu.VMEM(extra.shape, F32),
             pltpu.SemaphoreType.DMA((2 + nx // 2,)),
         ],
         compiler_params=params(28),
         name="step",
-    )(moments, base, gain, blocks, solid, pv, v0, v1, v2, pv_x, v0_x, v1_x, v2_x, xlo, xhi, rest_lo, rest_hi)
+    )(moments, base, gain, blocks, solid, pv, v0, v1, v2, pv_x, v0_x, v1_x, v2_x, xlo, xhi, e_other, e_mate)
 
 
 def solution(mesh):

time: 57.6 us -> 56.5 us (0.981)
  starting transfers between devices: 13.3 us -> 18.6 us
  blocking collectives: 25.7 us -> 22.2 us
  waiting for transfers between devices: 4.22 us -> 1.11 us
    ppermute x2 -> x3, starting transfers between devices: 0.12 us -> 4.47 us  [to_other(): lax.ppermute(block, 'gy', [(i, (i + (1 if i % 2 else -1)) % n) for i in r...]
    all_to_all x1, blocking collectives: 25.7 us -> 22.2 us  [local(): moments = lax.all_to_all(moments, ('gx', 'gy'), 0, 0, tiled=True)]
    ppermute x2, waiting for transfers between devices: 3.48 us -> 1.1 us  [shift(): lax.ppermute(block, axis, [(i, (i + distance) % n) for i in range(n)])]
    ppermute x2, starting transfers between devices: 5.04 us -> 6.57 us  [shift(): lax.ppermute(block, axis, [(i, (i + distance) % n) for i in range(n)])]
    ppermute x2 -> x3, waiting for transfers between devices: 0.74 us -> 0.01 us  [to_other(): lax.ppermute(block, 'gy', [(i, (i + (1 if i % 2 else -1)) % n) for i in r...]
    ppermute x2 -> x3, starting transfers between devices: 8.12 us -> 7.6 us  [to_mate(): return lax.ppermute(block, 'gy', [(i, i ^ 1) for i in range(n)])]
  transfers between devices with their start and end apart: 6 -> 8, of which waited for: 2 -> 1; matrix products, arithmetic and copies ran while one was open for 0% -> 0% of each run, Pallas kernels for 9% -> 14%
where the time goes in v4:
time: 56.5 us; the launch traced here: 56.4 us
  blocking collectives  22.2 us (39%)
  starting transfers between devices  18.6 us (33%)
  Pallas kernels  13.6 us (24%)
  waiting for transfers between devices  1.11 us (2%)
  between operations  0.87 us (2%)
    all_to_all x1, blocking collectives, local(): moments = lax.all_to_all(moments, ('gx', 'gy'), 0, 0, tiled=True)  22.2 us
    ppermute x3, starting transfers between devices, to_mate(): return lax.ppermute(block, 'gy', [(i, i ^ 1) for i in range(n)])  7.6 us
    ppermute x2, starting transfers between devices, shift(): lax.ppermute(block, axis, [(i, (i + distance) % n) for i in range(n)])  6.57 us
    ppermute x3, starting transfers between devices, to_other(): lax.ppermute(block, 'gy', [(i, (i + (1 if i % 2 else -1)) % n) for i in r...  4.47 us
    pallas_call x1, Pallas kernels, local(): pl.pallas_call(outer_kernel, out_shape=(edges,) * 4 + (jax.ShapeDtypeStru...  2.97 us
    pallas_call x1, Pallas kernels, local(): pl.pallas_call(step_kernel, out_shape=(brick, whole), in_specs=[VMEM] * 1...  2.97 us
    pallas_call x1, Pallas kernels, local(): pl.pallas_call(load_kernel, out_shape=(whole, brick, brick, brick, brick,...  2.52 us
    pallas_call x1, Pallas kernels, local(): pl.pallas_call(start_kernel, out_shape=(padded,) * 8, in_specs=[VMEM] * 6...  1.72 us
  transfers between devices with their start and end apart: 8, of which 1 were waited for; matrix products, arithmetic and copies ran while one was open for 0% of the time, Pallas kernels for 14%

profile of v4, /device:TPU:1, one launch (start us, length us, event | category | flops | bytes accessed | tf_op | source)
XLA Modules:
  0.0 56.4 jit_solution(3225192460441831147)
XLA Ops:
  0.6 2.5 %load.1 = (f32[2,7,16,8,512]{4,3,2,1,0:T(8,128)S(1)}, f32[16,8,512]{2,1,0:T(8,128)S(1)}, f32[16,8,512]{2,1,0:T(8,128)S(1)}, f32[16,8,512]{2,1,0:T(8,128)S(1)}, f...) custom-call(f32[2,7,16,8,512]{4,3,2,1,0:T(8,128)} %pops_hbm.1, ...), custom_call_target="tpu_custom_call" | custom-call | tf_op jit(solution)/shard_map/load/pallas_call | solution.py:534
  3.2 2.5 %collective-permute-start.2 = (f32[22,8,512]{2,1,0:T(8,128)S(1)}, f32[22,8,512]{2,1,0:T(8,128)S(1)}, u32[]{:S(2)}, u32[]{:S(2)}) collective-permute-start(f32[22,8,512]{2,1,0:T(8,128)S(1)} %get-tuple-element.57), channel_id=1, source_target_pairs={{0,32},{32,64},{64,96},{96,128},{128,160},{160,192},{192,224},{224... | collective-permute-start | bytes 1081352 | tf_op jit(solution)/shard_map/ppermute | solution.py:520
  5.7 4.0 %collective-permute-start.3 = (f32[22,8,512]{2,1,0:T(8,128)S(1)}, f32[22,8,512]{2,1,0:T(8,128)S(1)}, u32[]{:S(2)}, u32[]{:S(2)}) collective-permute-start(f32[22,8,512]{2,1,0:T(8,128)S(1)} %get-tuple-element.58), channel_id=1, source_target_pairs={{0,224},{32,0},{64,32},{96,64},{128,96},{160,128},{192,160},{224,1... | collective-permute-start | bytes 1081352 | tf_op jit(solution)/shard_map/ppermute | solution.py:520
  9.7 2.1 %collective-permute-start = (f32[288,512]{1,0:T(8,128)S(1)}, f32[288,512]{1,0:T(8,128)S(1)}, u32[]{:S(2)}, u32[]{:S(2)}) collective-permute-start(f32[288,512]{1,0:T(8,128)S(1)} %get-tuple-element.44), channel_id=1, source_target_pairs={{0,31},{1,2},{2,1},{3,4},{4,3},{5,6},{6,5},{7,8},{8,7},{9,10},{10,... | collective-permute-start | bytes 1769480 | tf_op jit(solution)/shard_map/ppermute | solution.py:515
  11.8 3.3 %collective-permute-start.1 = (f32[288,512]{1,0:T(8,128)S(1)}, f32[288,512]{1,0:T(8,128)S(1)}, u32[]{:S(2)}, u32[]{:S(2)}) collective-permute-start(f32[288,512]{1,0:T(8,128)S(1)} %get-tuple-element.45), channel_id=1, source_target_pairs={{0,1},{1,0},{2,3},{3,2},{4,5},{5,4},{6,7},{7,6},{8,9},{9,8},{10,11... | collective-permute-start | bytes 1769480 | tf_op jit(solution)/shard_map/ppermute | solution.py:510
  15.1 1.6 %prepare.1 = (f32[2,7,16,8,512]{4,3,2,1,0:T(8,128)S(1)}, f32[2,6,16,8,512]{4,3,2,1,0:T(8,128)S(1)}, f32[6,16,8,512]{3,2,1,0:T(8,128)S(1)}) custom-call(f32[2,7,16,8,512]{4,3,2,1,0:T(8,128)S(1)} %get-tuple-element.61.pops, f32[16,8,512]{2,1,0:T(8,128)S(1)} %get-tuple-element.62.solids), custom_call_target="tpu_custom_call" | custom-call | tf_op jit(solution)/shard_map/prepare/pallas_call | solution.py:553
  16.7 1.1 %collective-permute-done.2.xlo = f32[22,8,512]{2,1,0:T(8,128)S(1)} collective-permute-done((f32[22,8,512]{2,1,0:T(8,128)S(1)}, f32[22,8,512]{2,1,0:T(8,128)S(1)}, u32[]{:S(2)}, u32[]{:S(2)}) %collective-permute-start.2) | collective-permute-done | bytes 360480 | tf_op jit(solution)/shard_map/ppermute | solution.py:520
  17.8 0.0 collective-permute-done.3.xhi
  17.8 0.1 corners.1
  17.9 2.4 %collective-permute-start.4 = (f32[8,8,512]{2,1,0:T(8,128)S(1)}, f32[8,8,512]{2,1,0:T(8,128)S(1)}, u32[]{:S(2)}, u32[]{:S(2)}) collective-permute-start(f32[8,8,512]{2,1,0:T(8,128)S(1)} %get-tuple-element.64), channel_id=1, source_target_pairs={{0,31},{1,2},{2,1},{3,4},{4,3},{5,6},{6,5},{7,8},{8,7},{9,10},{10,... | collective-permute-start | bytes 393224 | tf_op jit(solution)/shard_map/ppermute | solution.py:515
  20.3 3.0 %collective-permute-start.5 = (f32[8,8,512]{2,1,0:T(8,128)S(1)}, f32[8,8,512]{2,1,0:T(8,128)S(1)}, u32[]{:S(2)}, u32[]{:S(2)}) collective-permute-start(f32[8,8,512]{2,1,0:T(8,128)S(1)} %get-tuple-element.65), channel_id=1, source_target_pairs={{0,1},{1,0},{2,3},{3,2},{4,5},{5,4},{6,7},{7,6},{8,9},{9,8},{10,11... | collective-permute-start | bytes 393224 | tf_op jit(solution)/shard_map/ppermute | solution.py:510
  23.3 0.0 collective-permute-start.6
  23.3 0.0 collective-permute-done.other
  23.3 1.3 %collective-permute-start.7 = (f32[5,16,512]{2,1,0:T(8,128)S(1)}, f32[5,16,512]{2,1,0:T(8,128)S(1)}, u32[]{:S(2)}, u32[]{:S(2)}) collective-permute-start(f32[5,16,512]{2,1,0:T(8,128)S(1)} %get-tuple-element.68), channel_id=1, source_target_pairs={{0,1},{1,0},{2,3},{3,2},{4,5},{5,4},{6,7},{7,6},{8,9},{9,8},{10,11... | collective-permute-start | bytes 491528 | tf_op jit(solution)/shard_map/ppermute | solution.py:510
  24.6 0.0 collective-permute-done.1.mate
  24.6 1.7 %start.1 = (f32[26,24,512]{2,1,0:T(8,128)S(1)}, f32[26,24,512]{2,1,0:T(8,128)S(1)}, f32[26,24,512]{2,1,0:T(8,128)S(1)}, f32[26,24,512]{2,1,0:T(8,128)S(1)}, f32[...) custom-call(f32[16,8,512]{2,1,0:T(8,128)S(1)} %get-tuple-element.40., ...), custom_call_target="tpu_custom_call" | custom-call | flops 60000000 | bytes 20000000 | tf_op jit(solution)/shard_map/start/pallas_call | solution.py:564
  26.4 1.7 %inner.1 = (f32[26,24,512]{2,1,0:T(8,128)S(1)}, f32[26,24,512]{2,1,0:T(8,128)S(1)}, f32[6,8,512]{2,1,0:T(8,128)S(1)}) custom-call(f32[26,24,512]{2,1,0:T(8,128)S(1)} %get-tuple-element.47.sg.sg_in, f32[26,24,512]{2,1,0:T(8,128)S(1)} %get-tuple-element.48.un.un_in, f32[26,24,512]{2,1,0:T(8,128)S(1)} %get-tuple-element.49.wx.wx_in, ...), custom_call_target="tpu_custom_call" | custom-call | flops 60000000 | bytes 20000000 | tf_op jit(solution)/shard_map/inner/pallas_call | solution.py:588
  28.0 0.0 collective-permute-done.4.other
  28.1 0.0 collective-permute-done.5.mate
  28.1 3.0 %outer.1 = (f32[16,24,512]{2,1,0:T(8,128)S(1)}, f32[16,24,512]{2,1,0:T(8,128)S(1)}, f32[16,24,512]{2,1,0:T(8,128)S(1)}, f32[16,24,512]{2,1,0:T(8,128)S(1)}, f32[256,128]{1,0:T(8,128)S(1)}) custom-call(f32[26,24,512]{2,1,0:T(8,128)S(1)} %get-tuple-element.46.pv_in.pv, f32[26,24,512]{2,1,0:T(8,128)S(1)} %get-tuple-element.47.sg.sg_in, ...), custom_call_target="tpu_custom_call" | custom-call | flops 20000000000 | bytes 300000000 | tf_op jit(solution)/shard_map/outer/pallas_call | solution.py:600
  31.0 0.0 collective-permute-done.6.extra_other
  31.1 0.0 collective-permute-done.7.extra_mate
  31.1 22.2 %all_to_all.11 = f32[256,1,128]{2,1,0:T(1,128)S(1)} all-to-all(f32[256,1,128]{2,1,0:T(1,128)S(1)} %bitcast.5), channel_id=1, replica_groups=mesh['gx'=8,'gy'=32] {'gx','gy'}, dimensions={0} | all-to-all | bytes 262144 | tf_op jit(solution)/shard_map/all_to_all | solution.py:611
  53.3 3.0 %step.1 = (f32[16,8,512]{2,1,0:T(8,128)}, f32[2,7,16,8,512]{4,3,2,1,0:T(8,128)}) custom-call(f32[256,128]{1,0:T(8,128)S(1)} %bitcast.4, f32[2,7,16,8,512]{4,3,2,1,0:T(8,128)S(1)} %get-tuple-element.70.base, f32[2,6,16,8,512]{4,3,2,1,0:T(8,128)S(1)} %get-tuple-element.71.gain, f32[6,16,8,512]{3,2,1,0:T(8,128)S(1)} %get-tuple-element.63.blocks, ...), custom_call_target="tpu_custom_call" | custom-call | tf_op jit(solution)/shard_map/step/pallas_call | solution.py:612
Async XLA Ops:
  3.2 14.6 %collective-permute-start.2 = (f32[22,8,512]{2,1,0:T(8,128)S(1)}, f32[22,8,512]{2,1,0:T(8,128)S(1)}, u32[]{:S(2)}, u32[]{:S(2)}) collective-permute-start(f32[22,8,512]{2,1,0:T(8,128)S(1)} %get-tuple-element.57), channel_id=1, source_target_pairs={{0,32},{32,64},{64,96},{96,128},{128,160},{160,192},{192,224},{224... | collective-permute-start | bytes 1081352 | tf_op jit(solution)/shard_map/ppermute | solution.py:520
  5.7 12.1 %collective-permute-start.3 = (f32[22,8,512]{2,1,0:T(8,128)S(1)}, f32[22,8,512]{2,1,0:T(8,128)S(1)}, u32[]{:S(2)}, u32[]{:S(2)}) collective-permute-start(f32[22,8,512]{2,1,0:T(8,128)S(1)} %get-tuple-element.58), channel_id=1, source_target_pairs={{0,224},{32,0},{64,32},{96,64},{128,96},{160,128},{192,160},{224,1... | collective-permute-start | bytes 1081352 | tf_op jit(solution)/shard_map/ppermute | solution.py:520
  9.7 13.6 %collective-permute-start = (f32[288,512]{1,0:T(8,128)S(1)}, f32[288,512]{1,0:T(8,128)S(1)}, u32[]{:S(2)}, u32[]{:S(2)}) collective-permute-start(f32[288,512]{1,0:T(8,128)S(1)} %get-tuple-element.44), channel_id=1, source_target_pairs={{0,31},{1,2},{2,1},{3,4},{4,3},{5,6},{6,5},{7,8},{8,7},{9,10},{10,... | collective-permute-start | bytes 1769480 | tf_op jit(solution)/shard_map/ppermute | solution.py:515
  11.8 12.8 %collective-permute-start.1 = (f32[288,512]{1,0:T(8,128)S(1)}, f32[288,512]{1,0:T(8,128)S(1)}, u32[]{:S(2)}, u32[]{:S(2)}) collective-permute-start(f32[288,512]{1,0:T(8,128)S(1)} %get-tuple-element.45), channel_id=1, source_target_pairs={{0,1},{1,0},{2,3},{3,2},{4,5},{5,4},{6,7},{7,6},{8,9},{9,8},{10,11... | collective-permute-start | bytes 1769480 | tf_op jit(solution)/shard_map/ppermute | solution.py:510
  17.9 10.2 %collective-permute-start.4 = (f32[8,8,512]{2,1,0:T(8,128)S(1)}, f32[8,8,512]{2,1,0:T(8,128)S(1)}, u32[]{:S(2)}, u32[]{:S(2)}) collective-permute-start(f32[8,8,512]{2,1,0:T(8,128)S(1)} %get-tuple-element.64), channel_id=1, source_target_pairs={{0,31},{1,2},{2,1},{3,4},{4,3},{5,6},{6,5},{7,8},{8,7},{9,10},{10,... | collective-permute-start | bytes 393224 | tf_op jit(solution)/shard_map/ppermute | solution.py:515
  20.3 7.8 %collective-permute-start.5 = (f32[8,8,512]{2,1,0:T(8,128)S(1)}, f32[8,8,512]{2,1,0:T(8,128)S(1)}, u32[]{:S(2)}, u32[]{:S(2)}) collective-permute-start(f32[8,8,512]{2,1,0:T(8,128)S(1)} %get-tuple-element.65), channel_id=1, source_target_pairs={{0,1},{1,0},{2,3},{3,2},{4,5},{5,4},{6,7},{7,6},{8,9},{9,8},{10,11... | collective-permute-start | bytes 393224 | tf_op jit(solution)/shard_map/ppermute | solution.py:510
  23.3 7.8 %collective-permute-start.6 = (f32[5,16,512]{2,1,0:T(8,128)S(1)}, f32[5,16,512]{2,1,0:T(8,128)S(1)}, u32[]{:S(2)}, u32[]{:S(2)}) collective-permute-start(f32[5,16,512]{2,1,0:T(8,128)S(1)} %get-tuple-element.67), channel_id=1, source_target_pairs={{0,31},{1,2},{2,1},{3,4},{4,3},{5,6},{6,5},{7,8},{8,7},{9,10},{10,... | collective-permute-start | bytes 491528 | tf_op jit(solution)/shard_map/ppermute | solution.py:515
  23.3 7.8 %collective-permute-start.7 = (f32[5,16,512]{2,1,0:T(8,128)S(1)}, f32[5,16,512]{2,1,0:T(8,128)S(1)}, u32[]{:S(2)}, u32[]{:S(2)}) collective-permute-start(f32[5,16,512]{2,1,0:T(8,128)S(1)} %get-tuple-element.68), channel_id=1, source_target_pairs={{0,1},{1,0},{2,3},{3,2},{4,5},{5,4},{6,7},{7,6},{8,9},{9,8},{10,11... | collective-permute-start | bytes 491528 | tf_op jit(solution)/shard_map/ppermute | solution.py:510
